TPU v7x, 512 devices: a whole 4x4x16 slice. The times are simulated.
512 devices in a mesh: dp: 32 (over z, x_lo), ctx: 16 (over y, x_hi, core).
Axes of the slice: x: 4 (x_hi: 2, x_lo: 2; x = x_hi * 2 + x_lo), y: 4, z: 16, core: 2. Of those that a mesh axis runs over, the one named last changes fastest.
Arguments:
- primal: bfloat16 [32, 2048, 2048], P('dp', 'ctx'), may hold values from -6 to 6
- tangent: bfloat16 [32, 2048, 2048], P('dp', 'ctx'), may hold values from -6 to 6
- cotangent: bfloat16 [32, 2048, 2048], P('dp', 'ctx'), may hold values from -6 to 6
- impulse: float32 [2048, 2048], P(None, 'ctx'), may hold values from -2 to 2
Outputs:
- out_primal: bfloat16 [32, 2048, 2048], P('dp', 'ctx')
- out_tangent: bfloat16 [32, 2048, 2048], P('dp', 'ctx')
- input_cotangent: bfloat16 [32, 2048, 2048], P('dp', 'ctx')
- impulse_grad: float32 [2048, 2048], P(None, 'ctx')
All inputs are finite; a program needn't handle non-finite values.
Results may differ from a plain program's by a relative error of at most 0.001.
Values may be sent and summed in bfloat16 or wider, within the bound.
A program may use at most 128 MiB of HBM per device.

v0:
```python
import math

import jax
import jax.numpy as jnp
from jax import lax
from jax.sharding import PartitionSpec as P


def divisor_pair(length):
    total = 2 * length
    inner = 1
    for candidate in range(1, length + 1):
        if length % candidate == 0 and candidate * candidate <= total:
            inner = candidate
    return (total // inner, inner)


def build_tables(length):
    outer, inner = divisor_pair(length)
    total = outer * inner
    rows = length // inner
    freq = jnp.arange(outer, dtype=jnp.int32)[:, None, None]
    column = jnp.arange(inner, dtype=jnp.int32)[None, :, None]
    block = jnp.arange(rows, dtype=jnp.int32)[None, None, :]
    index = freq * (block * inner + column) % total
    angle = index.astype(jnp.float32) * (2.0 * math.pi / total)
    cosine, sine = (jnp.cos(angle), jnp.sin(angle))
    first = jnp.stack([jnp.stack([cosine, sine], 2), jnp.stack([-sine, cosine], 2)], 0)
    left = jnp.arange(inner, dtype=jnp.int32)[:, None]
    right = jnp.arange(inner, dtype=jnp.int32)[None, :]
    angle_two = (left * right % inner).astype(jnp.float32) * (2.0 * math.pi / inner)
    cos_two, sin_two = (jnp.cos(angle_two), jnp.sin(angle_two))
    second = jnp.stack([jnp.stack([cos_two, sin_two], 1), jnp.stack([-sin_two, cos_two], 1)], 0)
    return (first, second, total)


def forward_spectrum(stacked, first, second):
    parts, length, width = stacked.shape
    inner = first.shape[2]
    rows = first.shape[4]
    blocks = stacked.reshape(parts, rows, inner, width)
    middle = jnp.einsum(
        "akqbn,bnqc->akqc", first[:, :, :, :parts], blocks, precision=lax.Precision.HIGHEST
    )
    return jnp.einsum("ajbq,bkqc->akjc", second, middle, precision=lax.Precision.HIGHEST)


def inverse_signal(spectrum, first, second, total):
    inner = first.shape[2]
    rows = first.shape[4]
    width = spectrum.shape[3]
    middle = jnp.einsum("bjaq,bkjc->akqc", second, spectrum, precision=lax.Precision.HIGHEST)
    result = jnp.einsum("bkqan,bkqc->anqc", first, middle, precision=lax.Precision.HIGHEST)
    return result.reshape(2, rows * inner, width) / float(total)


def spectral_product(left, right, conjugate):
    left_re, left_im = (left[0], left[1])
    if conjugate:
        left_im = -left_im
    right_re, right_im = (right[0], right[1])
    return jnp.stack(
        [left_re * right_re - left_im * right_im, left_re * right_im + left_im * right_re], 0
    )


def local(primal, tangent, cotangent, impulse):
    length = impulse.shape[0]
    first, second, total = build_tables(length)
    seq_u, seq_du = (
        lax.all_to_all(primal, "ctx", split_axis=2, concat_axis=1, tiled=True),
        lax.all_to_all(tangent, "ctx", split_axis=2, concat_axis=1, tiled=True),
    )
    signal_u = seq_u[0].astype(jnp.float32)
    signal_du = seq_du[0].astype(jnp.float32)
    filter_spec = forward_spectrum(impulse[None], first, second)
    paired_spec = forward_spectrum(jnp.stack([signal_u, signal_du], 0), first, second)
    mixed_spec = forward_spectrum(jnp.stack([impulse, -signal_u], 0), first, second)
    forward_out = inverse_signal(
        spectral_product(filter_spec, paired_spec, False), first, second, total
    )
    result_u = forward_out[0:1].astype(jnp.bfloat16)
    result_du = forward_out[1:2].astype(jnp.bfloat16)
    back_u, back_du = (
        lax.all_to_all(result_u, "ctx", split_axis=1, concat_axis=2, tiled=True),
        lax.all_to_all(result_du, "ctx", split_axis=1, concat_axis=2, tiled=True),
    )
    seq_g = lax.all_to_all(cotangent, "ctx", split_axis=2, concat_axis=1, tiled=True)
    cot_spec = forward_spectrum(seq_g[0].astype(jnp.float32)[None], first, second)
    adjoint_out = inverse_signal(spectral_product(mixed_spec, cot_spec, True), first, second, total)
    result_g = adjoint_out[0:1].astype(jnp.bfloat16)
    partial_grad = adjoint_out[1]
    summed = lax.psum(partial_grad, "dp")
    scale = 1.0 / math.sqrt(lax.axis_size("dp") * length)
    back_g = lax.all_to_all(result_g, "ctx", split_axis=1, concat_axis=2, tiled=True)
    return (back_u, back_du, back_g, summed * scale)


def solution(mesh):
    placed = (P("dp", "ctx", None), P("dp", "ctx", None), P("dp", "ctx", None), P(None, "ctx"))
    return jax.shard_map(
        local,
        mesh=mesh,
        in_specs=placed,
        out_specs=(
            P("dp", "ctx", None),
            P("dp", "ctx", None),
            P("dp", "ctx", None),
            P(None, "ctx"),
        ),
        check_vma=False,
    )
```

profile of v0, /device:TPU:24, one launch (start us, length us, event | category | flops | bytes accessed | tf_op | source)
XLA Modules:
  0.0 502.7 jit_solution(16054825199146420431)
XLA Ops:
  7.2 2.4 copy.117
  10.1 11.5 %reduce = bf16[2048,128]{1,0:T(8,128)(2,1)S(1)} reduce(bf16[2048,1,128]{2,1,0:T(2,128)(2,1)S(1)} %bitcast.192, bf16[]{:T(256)} %broadcast.269), dimensions={1}, to_apply=%bitcast.164.reduce_sub_computation | reduce | bytes 1048578
  22.5 10.1 %all-to-all-start.1 = ((bf16[16,2,8192]{2,1,0:T(2,128)(2,1)}), bf16[16,2,8192]{2,1,0:T(2,128)(2,1)}, u32[]{:S(2)}, u32[]{:S(2)}) async-start(bf16[16,2,8192]{2,1,0:T(2,128)(2,1)} %reshape.273), calls=%async_computation.1 | async-start | bytes 1048576 | tf_op jit(solution)/shard_map/all_to_all | solution.py:72
  32.9 5.8 %fusion.81 = (f32[64,64,1,32]{0,3,1,2:T(8,128)S(1)}, f32[64,64,1,32]{0,3,1,2:T(8,128)}, f32[64,64,1,32]{0,3,1,2:T(8,128)}) fusion(s32[64,32]{1,0:T(8,128)S(1)} %iota_add_fusion), kind=kLoop, calls=%fused_computation.76 | loop fusion | flops 1966080 | bytes 1581056 | tf_op jit(solution)/shard_map/sin | solution.py:27
  39.5 11.5 %reduce.1 = bf16[2048,128]{1,0:T(8,128)(2,1)S(1)} reduce(bf16[2048,1,128]{2,1,0:T(2,128)(2,1)S(1)} %bitcast.197, bf16[]{:T(256)} %broadcast.269), dimensions={1}, to_apply=%bitcast.166.reduce_sub_computation | reduce | bytes 1048578
  52.0 2.4 copy.137
  54.4 12.3 %reduce.4 = bf16[2048,128]{1,0:T(8,128)(2,1)} reduce(bf16[2048,1,128]{2,1,0:T(2,128)(2,1)S(1)} %bitcast.198, bf16[]{:T(256)} %broadcast.269), dimensions={1}, to_apply=%bitcast.172.reduce_sub_computation | reduce | bytes 1048578
  66.7 2.0 reshape.281
  68.7 1.6 copy.134
  70.3 2.7 maximum_bitcast_fusion
  74.3 8.7 %convolution_bitcast_fusion = f32[2,64,64,128,1]{3,1,0,2,4:T(8,128)} fusion(f32[32,64,128,1]{2,1,0,3:T(8,128)S(1)} %bitcast.183, f32[1,64,64,2,32]{1,4,0,2,3:T(8,128)S(1)} %get-tuple-element.28, f32[1,64,64,2,32]{1,4,0,2,3:T(8,128)S(1)} %get-tuple-element.29), kind=kOutput, calls=%fused_computation.31 | convolution fusion | flops 402915328 | bytes 7340032 | tf_op jit(solution)/shard_map/akqbn,bnqc->akqc/dot_general | solution.py:42
  83.0 7.2 %all-to-all-start = ((bf16[16,2,8192]{2,1,0:T(2,128)(2,1)}), bf16[16,2,8192]{2,1,0:T(2,128)(2,1)}, u32[]{:S(2)}, u32[]{:S(2)}) async-start(bf16[16,2,8192]{2,1,0:T(2,128)(2,1)} %reshape.275), calls=%async_computation | async-start | bytes 1048576 | tf_op jit(solution)/shard_map/all_to_all | solution.py:71
  90.2 9.8 %fusion.34 = f32[2,64,64,128]{3,2,0,1:T(8,128)} fusion(f32[2,64,64,128,1]{3,1,0,2,4:T(8,128)} %convolution_bitcast_fusion, f32[1,64,2,64]{3,1,2,0:T(8,128)S(1)} %get-tuple-element.31, f32[1,64,2,64]{3,1,2,0:T(8,128)S(1)} %get-tuple-element.30), kind=kOutput, calls=%fused_computation.34 | convolution fusion | flops 1610629120 | bytes 8454144 | tf_op jit(solution)/shard_map/ajbq,bkqc->akjc/dot_general | solution.py:45
  100.0 2.2 reshape.274
  103.7 2.8 copy.121
  106.5 7.2 %all-to-all-start.4 = ((bf16[16,2,8192]{2,1,0:T(2,128)(2,1)}), bf16[16,2,8192]{2,1,0:T(2,128)(2,1)}, u32[]{:S(2)}, u32[]{:S(2)}) async-start(bf16[16,2,8192]{2,1,0:T(2,128)(2,1)} %reshape.281), calls=%async_computation.4 | async-start | bytes 1048576 | tf_op jit(solution)/shard_map/all_to_all | solution.py:88
  113.7 2.6 reshape.276
  117.8 2.1 copy_negate_fusion
  120.0 6.9 %fusion.28 = f32[2,64,64,128,1]{3,1,0,2,4:T(8,128)S(1)} fusion(f32[1,32,64,128]{3,1,0,2:T(8,128)S(1)} %copy-done.8, f32[1,32,64,128]{3,1,0,2:T(8,128)S(1)} %get-tuple-element.25, f32[1,64,64,2,32]{1,4,0,2,3:T(8,128)S(1)} %copy-done.1, f32[1,64,64,2,32]{1,4,0,2,3:T(8,128)S(1)} %get-tuple-element.28), kind=kOutput, calls=%fused_computation.32 | convolution fusion | flops 806354944 | bytes 8388608 | tf_op jit(solution)/shard_map/akqbn,bnqc->akqc/dot_general | solution.py:42
  126.9 6.7 %fusion.37 = f32[2,64,64,128]{3,2,0,1:T(8,128)S(1)} fusion(f32[2,64,64,128,1]{3,1,0,2,4:T(8,128)S(1)} %fusion.28, f32[1,64,2,64]{3,1,2,0:T(8,128)S(1)} %get-tuple-element.31, f32[1,64,2,64]{3,1,2,0:T(8,128)S(1)} %get-tuple-element.30), kind=kOutput, calls=%fused_computation.35 | convolution fusion | flops 1610629120 | bytes 8454144 | tf_op jit(solution)/shard_map/ajbq,bkqc->akjc/dot_general | solution.py:45
  133.7 1.4 multiply_subtract_fusion.1
  135.1 4.2 fusion.46
  139.3 6.7 %fusion.68 = bf16[2,32,64,128]{3,1,0,2:T(8,128)(2,1)S(1)} fusion(f32[2,64,64,128,1]{3,2,0,1,4:T(8,128)S(1)} %fusion.46, f32[1,64,64,2,32]{1,4,0,2,3:T(8,128)S(1)} %copy-done.1, f32[1,64,64,2,32]{1,4,0,2,3:T(8,128)S(1)} %get-tuple-element.28), kind=kOutput, calls=%fused_computation.63 | convolution fusion | flops 806879232 | bytes 7340032 | tf_op jit(solution)/shard_map/bkqan,bkqc->anqc/dot_general | solution.py:53
  147.1 8.9 %copy.254 = bf16[1,2048,128]{2,0,1:T(2,128)(2,1)} copy(bf16[1,2048,128]{2,1,0:T(8,128)(2,1)S(1)} %bitcast.201) | data formatting | bytes 1048576 | tf_op jit(solution)/shard_map/convert_element_type | solution.py:82
  156.0 13.3 %reduce.2 = bf16[2048,128]{1,0:T(8,128)(2,1)} reduce(bf16[2048,1,128]{2,1,0:T(2,128)(2,1)} %bitcast.195, bf16[]{:T(256)} %broadcast.269), dimensions={1}, to_apply=%bitcast.181.reduce_sub_computation | reduce | bytes 1048578
  169.3 2.0 reshape.277
  171.3 7.2 %all-to-all-start.2 = ((bf16[16,2,8192]{2,1,0:T(2,128)(2,1)}), bf16[16,2,8192]{2,1,0:T(2,128)(2,1)}, u32[]{:S(2)}, u32[]{:S(2)}) async-start(bf16[16,2,8192]{2,1,0:T(2,128)(2,1)} %reshape.277), calls=%async_computation.2 | async-start | bytes 1048576 | tf_op jit(solution)/shard_map/all_to_all | solution.py:85
  178.5 3.9 reshape.282
  182.4 2.1 copy.197
  184.5 2.0 copy.138
  186.5 4.9 convolution_bitcast_fusion.1
  191.5 6.5 %fusion.43 = f32[2,64,64,128]{3,2,0,1:T(8,128)S(1)} fusion(f32[2,64,64,128,1]{3,1,0,2,4:T(8,128)S(1)} %convolution_bitcast_fusion.1, f32[1,64,2,64]{3,1,2,0:T(8,128)S(1)} %get-tuple-element.31, f32[1,64,2,64]{3,1,2,0:T(8,128)S(1)} %get-tuple-element.30), kind=kOutput, calls=%fused_computation.37 | convolution fusion | flops 1610629120 | bytes 8454144 | tf_op jit(solution)/shard_map/ajbq,bkqc->akjc/dot_general | solution.py:45
  198.0 7.1 %fusion.31 = f32[2,64,64,128,1]{3,1,0,2,4:T(8,128)S(1)} fusion(f32[1,32,64,128]{3,1,0,2:T(8,128)S(1)} %get-tuple-element.24, f32[1,32,64,128]{3,1,0,2:T(8,128)S(1)} %copy-done.7, f32[1,64,64,2,32]{1,4,0,2,3:T(8,128)S(1)} %copy-done.2, f32[1,64,64,2,32]{1,4,0,2,3:T(8,128)S(1)} %get-tuple-element.28), kind=kOutput, calls=%fused_computation.33 | convolution fusion | flops 806354944 | bytes 8388608 | tf_op jit(solution)/shard_map/akqbn,bnqc->akqc/dot_general | solution.py:42
  205.1 6.5 %fusion.40 = f32[2,64,64,128]{3,2,0,1:T(8,128)S(1)} fusion(f32[2,64,64,128,1]{3,1,0,2,4:T(8,128)S(1)} %fusion.31, f32[1,64,2,64]{3,1,2,0:T(8,128)S(1)} %get-tuple-element.31, f32[1,64,2,64]{3,1,2,0:T(8,128)S(1)} %get-tuple-element.30), kind=kOutput, calls=%fused_computation.36 | convolution fusion | flops 1610629120 | bytes 8454144 | tf_op jit(solution)/shard_map/ajbq,bkqc->akjc/dot_general | solution.py:45
  211.7 1.7 multiply_subtract_fusion
  213.4 4.2 fusion.49
  217.5 6.5 %fusion.58 = f32[2,32,64,128]{3,1,0,2:T(8,128)S(1)} fusion(f32[2,64,64,128,1]{3,2,0,1,4:T(8,128)S(1)} %fusion.49, f32[1,64,64,2,32]{1,4,0,2,3:T(8,128)S(1)} %copy-done.2, f32[1,64,64,2,32]{1,4,0,2,3:T(8,128)S(1)} %get-tuple-element.28), kind=kOutput, calls=%fused_computation.53 | convolution fusion | flops 806354944 | bytes 8388608 | tf_op jit(solution)/shard_map/bkqan,bkqc->anqc/dot_general | solution.py:53
  224.2 1.6 copy.147
  226.0 8.5 %copy.253 = bf16[1,2048,128]{2,0,1:T(2,128)(2,1)S(1)} copy(bf16[1,2048,128]{2,1,0:T(8,128)(2,1)S(1)} %bitcast.204) | data formatting | bytes 1048576 | tf_op jit(solution)/shard_map/convert_element_type | solution.py:83
  234.5 11.5 %reduce.3 = bf16[2048,128]{1,0:T(8,128)(2,1)S(1)} reduce(bf16[2048,1,128]{2,1,0:T(2,128)(2,1)S(1)} %bitcast.196, bf16[]{:T(256)} %broadcast.269), dimensions={1}, to_apply=%bitcast.180.reduce_sub_computation | reduce | bytes 1048578
  247.0 7.5 %all-to-all-start.3 = ((bf16[16,2,8192]{2,1,0:T(2,128)(2,1)}), bf16[16,2,8192]{2,1,0:T(2,128)(2,1)S(1)}, u32[]{:S(2)}, u32[]{:S(2)}) async-start(bf16[16,2,8192]{2,1,0:T(2,128)(2,1)} %reshape.279), calls=%async_computation.3 | async-start | bytes 1048576 | tf_op jit(solution)/shard_map/all_to_all | solution.py:86
  256.0 8.1 %copy.252 = bf16[1,2048,128]{2,0,1:T(2,128)(2,1)S(1)} copy(bf16[1,2048,128]{2,1,0:T(8,128)(2,1)S(1)} %bitcast.205) | data formatting | bytes 1048576 | tf_op jit(solution)/shard_map/convert_element_type | solution.py:91
  264.2 11.5 %reduce.5 = bf16[2048,128]{1,0:T(8,128)(2,1)S(1)} reduce(bf16[2048,1,128]{2,1,0:T(2,128)(2,1)S(1)} %bitcast.193, bf16[]{:T(256)} %broadcast.269), dimensions={1}, to_apply=%bitcast.179.reduce_sub_computation | reduce | bytes 1048578
  276.6 7.2 %all-to-all-start.5 = ((bf16[16,2,8192]{2,1,0:T(2,128)(2,1)}), bf16[16,2,8192]{2,1,0:T(2,128)(2,1)S(1)}, u32[]{:S(2)}, u32[]{:S(2)}) async-start(bf16[16,2,8192]{2,1,0:T(2,128)(2,1)} %reshape.283), calls=%async_computation.5 | async-start | bytes 1048576 | tf_op jit(solution)/shard_map/all_to_all | solution.py:95
  283.8 2.2 reshape.278
  289.3 6.2 %all-to-all-done.5 = bf16[16,2,8192]{2,1,0:T(2,128)(2,1)S(1)} async-done(((bf16[16,2,8192]{2,1,0:T(2,128)(2,1)}), bf16[16,2,8192]{2,1,0:T(2,128)(2,1)S(1)}, u32[]{:S(2)}, u32[]{:S(2)}) %all-to-all-start.5) | async-done | bytes 524320 | tf_op jit(solution)/shard_map/all_to_all | solution.py:95
  297.4 196.0 %all-reduce.2.cloned.1.call-done = f32[2048,128]{1,0:T(8,128)} async-done(((f32[2048,128]{1,0:T(8,128)}), f32[2048,128]{1,0:T(8,128)}) %all-reduce.2.cloned.1.call-update) | async-done | bytes 1048592 | tf_op jit(solution)/shard_map/psum | solution.py:93
  493.4 2.3 broadcast_multiply_fusion
  (63 shorter events, 17.8 us)
Async XLA Ops:
  22.5 16.3 %copy-start.10 = (bf16[1,128,2048]{2,1,0:T(8,128)(2,1)S(1)}, bf16[1,128,2048]{2,1,0:T(8,128)(2,1)}, u32[]{:S(2)}) copy-start(bf16[1,128,2048]{2,1,0:T(8,128)(2,1)} %param.4) | copy-start | bytes 1572868
  22.5 60.5 %all-to-all-start.1 = ((bf16[16,2,8192]{2,1,0:T(2,128)(2,1)}), bf16[16,2,8192]{2,1,0:T(2,128)(2,1)}, u32[]{:S(2)}, u32[]{:S(2)}) async-start(bf16[16,2,8192]{2,1,0:T(2,128)(2,1)} %reshape.273), calls=%async_computation.1 | async-start | bytes 1048576 | tf_op jit(solution)/shard_map/all_to_all | solution.py:72
  52.0 16.7 %copy-start.5 = (f32[2048,128]{1,0:T(8,128)S(1)}, f32[2048,128]{1,0:T(8,128)}, u32[]{:S(2)}) copy-start(f32[2048,128]{1,0:T(8,128)} %param.7) | copy-start | bytes 3145732
  70.3 4.0 copy-start.6
  73.0 1.4 copy-start
  83.0 23.5 %all-to-all-start = ((bf16[16,2,8192]{2,1,0:T(2,128)(2,1)}), bf16[16,2,8192]{2,1,0:T(2,128)(2,1)}, u32[]{:S(2)}, u32[]{:S(2)}) async-start(bf16[16,2,8192]{2,1,0:T(2,128)(2,1)} %reshape.275), calls=%async_computation | async-start | bytes 1048576 | tf_op jit(solution)/shard_map/all_to_all | solution.py:71
  106.5 64.8 %all-to-all-start.4 = ((bf16[16,2,8192]{2,1,0:T(2,128)(2,1)}), bf16[16,2,8192]{2,1,0:T(2,128)(2,1)}, u32[]{:S(2)}, u32[]{:S(2)}) async-start(bf16[16,2,8192]{2,1,0:T(2,128)(2,1)} %reshape.281), calls=%async_computation.4 | async-start | bytes 1048576 | tf_op jit(solution)/shard_map/all_to_all | solution.py:88
  117.8 2.1 copy-start.1
  117.8 2.2 copy-start.8
  126.9 6.8 %copy-start.3 = (f32[2,64,64,128]{3,2,0,1:T(8,128)S(1)}, f32[2,64,64,128]{3,2,0,1:T(8,128)}, u32[]{:S(2)}) copy-start(f32[2,64,64,128]{3,2,0,1:T(8,128)} %fusion.34) | copy-start | bytes 12582916
  171.3 75.7 %all-to-all-start.2 = ((bf16[16,2,8192]{2,1,0:T(2,128)(2,1)}), bf16[16,2,8192]{2,1,0:T(2,128)(2,1)}, u32[]{:S(2)}, u32[]{:S(2)}) async-start(bf16[16,2,8192]{2,1,0:T(2,128)(2,1)} %reshape.277), calls=%async_computation.2 | async-start | bytes 1048576 | tf_op jit(solution)/shard_map/all_to_all | solution.py:85
  178.5 314.9 %all-reduce.2.cloned.1.call-start = ((), (), s32[]{:S(2)}) async-start(), calls=%async_computation.6 | async-start | bytes 2097152 | tf_op jit(solution)/shard_map/psum | solution.py:93
  191.4 6.6 %copy-start.2 = (f32[1,64,64,2,32]{1,4,0,2,3:T(8,128)S(1)}, f32[1,64,64,2,32]{1,4,0,2,3:T(8,128)}, u32[]{:S(2)}) copy-start(f32[1,64,64,2,32]{1,4,0,2,3:T(8,128)} %copy-done) | copy-start | bytes 3145732
  191.5 6.6 %copy-start.7 = (f32[1,32,64,128]{3,1,0,2:T(8,128)S(1)}, f32[1,32,64,128]{3,1,0,2:T(8,128)}, u32[]{:S(2)}) copy-start(f32[1,32,64,128]{3,1,0,2:T(8,128)} %copy.134) | copy-start | bytes 3145732
  224.1 1.7 copy-start.4
  224.1 1.6 copy-start.9
  247.0 29.6 %all-to-all-start.3 = ((bf16[16,2,8192]{2,1,0:T(2,128)(2,1)}), bf16[16,2,8192]{2,1,0:T(2,128)(2,1)S(1)}, u32[]{:S(2)}, u32[]{:S(2)}) async-start(bf16[16,2,8192]{2,1,0:T(2,128)(2,1)} %reshape.279), calls=%async_computation.3 | async-start | bytes 1048576 | tf_op jit(solution)/shard_map/all_to_all | solution.py:86
  276.6 18.9 %all-to-all-start.5 = ((bf16[16,2,8192]{2,1,0:T(2,128)(2,1)}), bf16[16,2,8192]{2,1,0:T(2,128)(2,1)S(1)}, u32[]{:S(2)}, u32[]{:S(2)}) async-start(bf16[16,2,8192]{2,1,0:T(2,128)(2,1)} %reshape.283), calls=%async_computation.5 | async-start | bytes 1048576 | tf_op jit(solution)/shard_map/all_to_all | solution.py:95
Sparse Core Ops, SparseCore 0:
  225.9 267.4 all-reduce.1
where the time goes:
time: 508 us; the launch traced here: 503 us
  waiting for transfers between devices  202 us (40%)
  other arithmetic  88 us (17%)
  matrix products  78.7 us (15%)
  local copies, waits for them, and re-layouts  72.6 us (14%)
  starting transfers between devices  46.5 us (9%)
  between operations  14.7 us (3%)
    psum x1, waiting for transfers between devices, local(): summed = lax.psum(partial_grad, 'dp')  196 us
    unnamed x6, other arithmetic  71.6 us
    unnamed x45, local copies, waits for them, and re-layouts  32.5 us
    dot_general x4, matrix products, forward_spectrum(): jnp.einsum('ajbq,bkqc->akjc', second, middle, precision=lax.Precision.HIG...  29.6 us
    dot_general x4, matrix products, forward_spectrum(): jnp.einsum('akqbn,bnqc->akqc', first[:, :, :, :parts], blocks, precision=...  27.6 us
    dot_general x2, matrix products, inverse_signal(): jnp.einsum('bkqan,bkqc->anqc', first, middle, precision=lax.Precision.HIG...  13.2 us
  transfers between devices with their start and end apart: 7, of which 2 were waited for; matrix products, arithmetic and copies ran while one was open for 44% of the time, Pallas kernels for 0%

commit v1 on v0

v1 whole, which is shorter than its diff:
```python
import functools
import math

import jax
import jax.numpy as jnp
import ml_dtypes
import numpy as np
from jax import lax
from jax.experimental import pallas as pl
from jax.experimental.pallas import tpu as pltpu
from jax.sharding import PartitionSpec as P

MESH = pl.DeviceIdType.MESH
LANES = 128
SPLIT = 16
MIB = 1024 * 1024


def two_pieces(table):
    high = table.astype(ml_dtypes.bfloat16)
    low = (table - high.astype(np.float64)).astype(ml_dtypes.bfloat16)
    return high, low


def build_tables(length):
    total = 2 * length
    rows = length // SPLIT
    time = np.arange(rows)[None, :] * SPLIT + np.arange(SPLIT)[:, None]
    angle = 2.0 * np.pi * (time[:, None, :] * np.arange(rows)[None, :, None] % total) / total
    real, imag = np.cos(angle), -np.sin(angle)
    real[:, 0, :] = 1.0
    imag[:, 0, :] = 1.0 - 2.0 * (np.arange(rows) % 2)
    high, low = two_pieces(np.concatenate([real, imag], 1))
    analysis = np.concatenate([high, low], 2)
    real, imag = np.cos(angle) * (2.0 / total), -np.sin(angle) * (2.0 / total)
    real[:, 0, :] = (np.arange(rows) % 2 == 0)[None, :]
    imag[:, 0, :] = (np.arange(rows) % 2 == 1)[None, :]
    high, low = two_pieces(np.concatenate([real, imag], 1).transpose(0, 2, 1))
    synthesis = np.concatenate([high, low], 1)
    edge = np.zeros((2 * SPLIT, 2 * SPLIT))
    back = np.zeros((2 * SPLIT, 2 * SPLIT))
    point = np.arange(SPLIT)
    folded = np.arange(2 * SPLIT)
    for m in range(SPLIT):
        turn = 2.0 * np.pi * m * point / (2 * SPLIT)
        start = SPLIT * (m % 2)
        edge[m, start : start + SPLIT] = np.cos(turn)
        full = 2.0 * np.pi * m * folded / (2 * SPLIT)
        if m:
            edge[SPLIT + m, start : start + SPLIT] = -np.sin(turn)
            back[:, m] = 2.0 * np.cos(full) / total
            back[:, SPLIT + m] = -2.0 * np.sin(full) / total
    edge[SPLIT, :SPLIT] = np.cos(np.pi * point)
    back[:, 0] = 1.0 / total
    back[:, SPLIT] = np.cos(np.pi * folded) / total
    return analysis, synthesis, edge.astype(np.float32), back.astype(np.float32)


def times(value, power, sign):
    re, im = value
    power = (power * sign) % 16
    if power == 0:
        return (re, im)
    if power == 4:
        return (-im, re)
    if power == 8:
        return (-re, -im)
    if power == 12:
        return (im, -re)
    c, s = math.cos(math.pi * power / 8), math.sin(math.pi * power / 8)
    if power % 4 == 2:
        size = math.sqrt(0.5)
        if power == 2:
            return ((re - im) * size, (re + im) * size)
        if power == 6:
            return ((re + im) * -size, (re - im) * size)
        if power == 10:
            return ((im - re) * size, (re + im) * -size)
        return ((re + im) * size, (im - re) * size)
    return (re * c - im * s, re * s + im * c)


def four(a, b, c, d, sign):
    sr, si = a[0] + c[0], a[1] + c[1]
    dr, di = a[0] - c[0], a[1] - c[1]
    tr, ti = b[0] + d[0], b[1] + d[1]
    er, ei = b[0] - d[0], b[1] - d[1]
    plus = (dr - ei, di + er)
    minus = (dr + ei, di - er)
    if sign < 0:
        plus, minus = minus, plus
    return ((sr + tr, si + ti), plus, (sr - tr, si - ti), minus)


def sixteen(points, sign):
    inner = [four(points[b], points[4 + b], points[8 + b], points[12 + b], sign) for b in range(4)]
    result = [None] * 16
    for c in range(4):
        column = [times(inner[b][c], b * c, sign) for b in range(4)]
        outer = four(*column, sign)
        for d in range(4):
            result[c + 4 * d] = outer[d]
    return result


def product(a, b, conjugate):
    if conjugate:
        return (a[0] * b[0] + a[1] * b[1], a[0] * b[1] - a[1] * b[0])
    return (a[0] * b[0] - a[1] * b[1], a[0] * b[1] + a[1] * b[0])


U, DU, G, H = range(4)
PAIRS = ((H, U, False), (H, DU, False), (H, G, True), (U, G, True))


def lanes(index):
    return slice(index * LANES, (index + 1) * LANES)


def transform_kernel(
    u_ref, du_ref, g_ref, h_ref, analysis, synthesis, edge, back,
    ou_ref, odu_ref, og_ref, grad_ref,
    signal, spec, prod, rim, rim_out,
):
    length = h_ref.shape[0]
    rows = length // SPLIT
    signal[U] = u_ref[...].astype(jnp.float32)
    signal[DU] = du_ref[...].astype(jnp.float32)
    signal[G] = g_ref[...].astype(jnp.float32)
    high = h_ref[...].astype(jnp.bfloat16).astype(jnp.float32)
    signal[H] = high
    signal[H + 1] = h_ref[...] - high

    for q in range(SPLIT):
        pieces = [signal[s, pl.ds(q, rows, stride=SPLIT), :].astype(jnp.bfloat16) for s in range(5)]
        block = jnp.concatenate(pieces, 1)
        block = jnp.concatenate([block, block], 0)
        out = jnp.dot(analysis[q], block, preferred_element_type=jnp.float32)
        parts = [out[:, lanes(s)] for s in range(3)] + [out[:, lanes(3)] + out[:, lanes(4)]]
        for s in range(4):
            spec[s, q] = parts[s]
            rim[q : q + 1, lanes(s)] = parts[s][0:1]
            rim[SPLIT + q : SPLIT + q + 1, lanes(s)] = parts[s][rows : rows + 1]

    rims = jnp.dot(
        edge[...], rim[...], precision=lax.Precision.HIGHEST, preferred_element_type=jnp.float32
    )
    first = lax.broadcasted_iota(jnp.int32, (SPLIT, LANES), 0) == 0
    for o, (a, b, conjugate) in enumerate(PAIRS):
        left = (rims[:SPLIT, lanes(a)], rims[SPLIT:, lanes(a)])
        right = (rims[:SPLIT, lanes(b)], rims[SPLIT:, lanes(b)])
        re, im = product(left, right, conjugate)
        rim[:SPLIT, lanes(o)] = jnp.where(first, left[0] * right[0], re)
        rim[SPLIT:, lanes(o)] = jnp.where(first, left[1] * right[1], im)
    rim_out[...] = jnp.dot(
        back[...], rim[...], precision=lax.Precision.HIGHEST, preferred_element_type=jnp.float32
    )

    @pl.loop(0, rows // 8)
    def _(tile):
        upper = pl.ds(pl.multiple_of(tile * 8, 8), 8)
        lower = pl.ds(pl.multiple_of(rows + tile * 8, 8), 8)
        for s in range(4):
            found = sixteen([(spec[s, q, upper, :], spec[s, q, lower, :]) for q in range(SPLIT)], -1)
            for j in range(SPLIT):
                spec[s, j, upper, :] = found[j][0]
                spec[s, j, lower, :] = found[j][1]
        for o, (a, b, conjugate) in enumerate(PAIRS):
            mixed = [
                product(
                    (spec[a, j, upper, :], spec[a, j, lower, :]),
                    (spec[b, j, upper, :], spec[b, j, lower, :]),
                    conjugate,
                )
                for j in range(SPLIT)
            ]
            found = sixteen(mixed, 1)
            for q in range(SPLIT):
                prod[o, q, upper, :] = found[q][0]
                prod[o, q, lower, :] = found[q][1]

    for q in range(SPLIT):
        for o in range(4):
            prod[o, q, 0:1, :] = rim_out[q : q + 1, lanes(o)]
            prod[o, q, rows : rows + 1, :] = rim_out[SPLIT + q : SPLIT + q + 1, lanes(o)]

    for q in range(SPLIT):
        block = jnp.concatenate([prod[o, q] for o in range(4)], 1)
        top = block.astype(jnp.bfloat16)
        rest = (block - top.astype(jnp.float32)).astype(jnp.bfloat16)
        both = jnp.dot(synthesis[q], top, preferred_element_type=jnp.float32)
        more = jnp.dot(synthesis[q, :rows], rest, preferred_element_type=jnp.float32)
        out = both[:rows] + (both[rows:] + more)
        for o in range(4):
            signal[o, pl.ds(q, rows, stride=SPLIT), :] = out[:, lanes(o)]

    ou_ref[...] = signal[U].astype(jnp.bfloat16)
    odu_ref[...] = signal[DU].astype(jnp.bfloat16)
    og_ref[...] = signal[G].astype(jnp.bfloat16)
    grad_ref[...] = signal[3]


def transform(u, du, g, h, tables):
    length, width = h.shape
    rows = length // SPLIT
    whole = pl.BlockSpec(memory_space=pltpu.VMEM)
    half = jax.ShapeDtypeStruct((length, width), jnp.bfloat16)
    return pl.pallas_call(
        transform_kernel,
        out_shape=(half, half, half, jax.ShapeDtypeStruct((length, width), jnp.float32)),
        in_specs=[whole] * 8,
        out_specs=(whole,) * 4,
        scratch_shapes=[
            pltpu.VMEM((5, length, width), jnp.float32),
            pltpu.VMEM((4, SPLIT, 2 * rows, width), jnp.float32),
            pltpu.VMEM((4, SPLIT, 2 * rows, width), jnp.float32),
            pltpu.VMEM((2 * SPLIT, 4 * width), jnp.float32),
            pltpu.VMEM((2 * SPLIT, 4 * width), jnp.float32),
        ],
        compiler_params=pltpu.CompilerParams(vmem_limit_bytes=48 * MIB),
        name="transform",
    )(u, du, g, h, *tables)


def gather_kernel(n, a_ref, b_ref, c_ref, oa_ref, ob_ref, oc_ref, local_sem, send_sem, recv_sem):
    me = lax.axis_index("ctx")
    barrier = pltpu.get_barrier_semaphore()
    for step in range(1, n):
        pl.semaphore_signal(
            barrier, inc=1, device_id={"ctx": lax.rem(me + step, n)}, device_id_type=MESH
        )
    pl.semaphore_wait(barrier, n - 1)
    tokens = a_ref.shape[1]
    mine = pl.ds(pl.multiple_of(me * tokens, tokens), tokens)
    own = pl.ds(pl.multiple_of(me * LANES, LANES), LANES)
    copies = []
    for i, (src, dst) in enumerate(((a_ref, oa_ref), (b_ref, ob_ref), (c_ref, oc_ref))):
        for step in range(1, n):
            other = lax.rem(me + step, n)
            copy = pltpu.make_async_remote_copy(
                src_ref=src.at[0, :, pl.ds(pl.multiple_of(other * LANES, LANES), LANES)],
                dst_ref=dst.at[mine, :],
                send_sem=send_sem.at[i, step],
                recv_sem=recv_sem.at[i, step],
                device_id={"ctx": other},
                device_id_type=MESH,
            )
            copy.start()
            copies.append(copy)
        copy = pltpu.make_async_copy(src.at[0, :, own], dst.at[mine, :], local_sem.at[i])
        copy.start()
        copies.append(copy)
    for copy in copies:
        copy.wait()


def gather_tokens(a, b, c):
    n = lax.axis_size("ctx")
    length = n * a.shape[1]
    anywhere = pl.BlockSpec(memory_space=pl.ANY)
    shape = jax.ShapeDtypeStruct((length, LANES), jnp.bfloat16)
    return pl.pallas_call(
        functools.partial(gather_kernel, n),
        out_shape=(shape,) * 3,
        in_specs=[anywhere] * 3,
        out_specs=(anywhere,) * 3,
        scratch_shapes=[
            pltpu.SemaphoreType.DMA((3,)),
            pltpu.SemaphoreType.DMA((3, n)),
            pltpu.SemaphoreType.DMA((3, n)),
        ],
        compiler_params=pltpu.CompilerParams(collective_id=0, has_side_effects=True),
        name="gather_tokens",
    )(a, b, c)


def scatter_kernel(
    n, rings, a_ref, b_ref, c_ref, part_ref, oa_ref, ob_ref, oc_ref, grad_ref,
    right_box, left_box, pair_out, pair_in,
    local_sem, send_sem, recv_sem, right_send, right_recv, left_send, left_recv, pair_sem,
    right_send2, right_recv2, left_send2, left_recv2,
):
    me = lax.axis_index("ctx")
    dp = lax.axis_index("dp")
    z, x = lax.div(dp, 2), lax.rem(dp, 2)
    up = {"dp": lax.rem(z + 1, rings) * 2 + x}
    down = {"dp": lax.rem(z + rings - 1, rings) * 2 + x}
    twin = {"dp": z * 2 + 1 - x}
    barrier = pltpu.get_barrier_semaphore()
    for step in range(1, n):
        pl.semaphore_signal(
            barrier, inc=1, device_id={"ctx": lax.rem(me + step, n)}, device_id_type=MESH
        )
    for device in (up, down, twin):
        pl.semaphore_signal(barrier, inc=1, device_id=device, device_id_type=MESH)
    pl.semaphore_wait(barrier, n + 2)

    tokens = oa_ref.shape[1]
    rows = part_ref.shape[0] // rings
    far, near = rings // 2, rings // 2 - 1

    def chunk(index):
        place = lax.rem(index + 2 * rings, rings)
        return pl.ds(pl.multiple_of(place * rows, rows), rows)

    def send(src, dst, sends, recvs, step, device):
        copy = pltpu.make_async_remote_copy(
            src_ref=src, dst_ref=dst, send_sem=sends.at[step], recv_sem=recvs.at[step],
            device_id=device, device_id_type=MESH,
        )
        copy.start()
        return copy

    started = []
    right = send(part_ref.at[chunk(z + far), :], right_box.at[0], right_send, right_recv, 0, up)
    left = send(part_ref.at[chunk(z - near), :], left_box.at[0], left_send, left_recv, 0, down)
    started += [right, left]

    own = pl.ds(pl.multiple_of(me * LANES, LANES), LANES)
    mine = pl.ds(pl.multiple_of(me * tokens, tokens), tokens)
    copies = []
    for i, (src, dst) in enumerate(((a_ref, oa_ref), (b_ref, ob_ref), (c_ref, oc_ref))):
        for step in range(1, n):
            other = lax.rem(me + step, n)
            copy = pltpu.make_async_remote_copy(
                src_ref=src.at[pl.ds(pl.multiple_of(other * tokens, tokens), tokens), :],
                dst_ref=dst.at[0, :, own],
                send_sem=send_sem.at[i, step],
                recv_sem=recv_sem.at[i, step],
                device_id={"ctx": other},
                device_id_type=MESH,
            )
            copy.start()
            copies.append(copy)
        copy = pltpu.make_async_copy(src.at[mine, :], dst.at[0, :, own], local_sem.at[i])
        copy.start()
        copies.append(copy)

    for step in range(1, far):
        right.wait_recv()
        right_box[step - 1] += part_ref[chunk(z + far - step), :]
        right = send(right_box.at[step - 1], right_box.at[step], right_send, right_recv, step, up)
        started.append(right)
        if step < near:
            left.wait_recv()
            left_box[step - 1] += part_ref[chunk(z - near + step), :]
            left = send(left_box.at[step - 1], left_box.at[step], left_send, left_recv, step, down)
            started.append(left)
    left.wait_recv()
    right.wait_recv()
    pair_out[...] = part_ref[chunk(z), :] + (right_box[far - 1] + left_box[near - 1])
    pair = pltpu.make_async_remote_copy(
        src_ref=pair_out, dst_ref=pair_in, send_sem=pair_sem.at[0], recv_sem=pair_sem.at[1],
        device_id=twin, device_id_type=MESH,
    )
    pair.start()
    pair.wait_recv()
    grad_ref[chunk(z), :] = pair_out[...] + pair_in[...]
    for step in range(far):
        if step:
            right.wait_recv()
        place = chunk(z - step)
        right = send(grad_ref.at[place, :], grad_ref.at[place, :], right_send2, right_recv2, step, up)
        started.append(right)
        if step < near:
            if step:
                left.wait_recv()
            place = chunk(z + step)
            left = send(grad_ref.at[place, :], grad_ref.at[place, :], left_send2, left_recv2, step, down)
            started.append(left)
    right.wait_recv()
    left.wait_recv()
    pair.wait_send()
    for copy in started:
        copy.wait_send()
    for copy in copies:
        copy.wait()


def scatter_tokens(a, b, c, part):
    n = lax.axis_size("ctx")
    rings = lax.axis_size("dp") // 2
    length, width = part.shape
    far, near = rings // 2, rings // 2 - 1
    anywhere = pl.BlockSpec(memory_space=pl.ANY)
    whole = pl.BlockSpec(memory_space=pltpu.VMEM)
    shape = jax.ShapeDtypeStruct((1, length // n, n * width), jnp.bfloat16)
    box = (length // rings, width)
    sem = pltpu.SemaphoreType.DMA
    return pl.pallas_call(
        functools.partial(scatter_kernel, n, rings),
        out_shape=(shape,) * 3 + (jax.ShapeDtypeStruct((length, width), jnp.float32),),
        in_specs=[anywhere] * 3 + [whole],
        out_specs=(anywhere,) * 3 + (whole,),
        scratch_shapes=[
            pltpu.VMEM((far,) + box, jnp.float32),
            pltpu.VMEM((near,) + box, jnp.float32),
            pltpu.VMEM(box, jnp.float32),
            pltpu.VMEM(box, jnp.float32),
            sem((3,)), sem((3, n)), sem((3, n)),
            sem((far,)), sem((far,)), sem((near,)), sem((near,)), sem((2,)),
            sem((far,)), sem((far,)), sem((near,)), sem((near,)),
        ],
        compiler_params=pltpu.CompilerParams(
            collective_id=1, has_side_effects=True, vmem_limit_bytes=32 * MIB
        ),
        name="scatter_tokens",
    )(a, b, c, part)


def local(primal, tangent, cotangent, impulse):
    length = impulse.shape[0]
    tables = [jnp.asarray(t) for t in build_tables(length)]
    u, g, du = gather_tokens(primal, cotangent, tangent)
    out_u, out_du, out_g, part = transform(u, du, g, impulse, tables)
    back_u, back_du, back_g, summed = scatter_tokens(out_u, out_du, out_g, part)
    scale = 1.0 / math.sqrt(lax.axis_size("dp") * length)
    return (back_u, back_du, back_g, summed * scale)


def solution(mesh):
    placed = (P("dp", "ctx", None), P("dp", "ctx", None), P("dp", "ctx", None), P(None, "ctx"))
    return jax.shard_map(
        local,
        mesh=mesh,
        in_specs=placed,
        out_specs=(
            P("dp", "ctx", None),
            P("dp", "ctx", None),
            P("dp", "ctx", None),
            P(None, "ctx"),
        ),
        check_vma=False,
    )
```

time: 508 us -> 124 us (0.24)
  the two profiles are of different devices: /device:TPU:24 before, /device:TPU:2 now
where the time goes in v1:
time: 124 us
  Pallas kernels  115 us (93%)
  local copies, waits for them, and re-layouts  6.93 us (6%)
    pallas_call x1, Pallas kernels, scatter_tokens(): pl.pallas_call(functools.partial(scatter_kernel, n, rings), out_shape=(sh...  73.7 us
    pallas_call x1, Pallas kernels, gather_tokens(): pl.pallas_call(functools.partial(gather_kernel, n), out_shape=(shape,) *...  25.9 us
    pallas_call x1, Pallas kernels, transform(): pl.pallas_call(transform_kernel, out_shape=(half, half, half, jax.ShapeDt...  15.4 us
    unnamed x15, local copies, waits for them, and re-layouts  6.93 us

profile of v1, /device:TPU:2, one launch (start us, length us, event | category | flops | bytes accessed | tf_op | source)
XLA Modules:
  0.0 123.7 jit_solution(16327946370579561275)
XLA Ops:
  0.6 0.0 copy-start
  0.6 25.9 %gather_tokens.1 = (bf16[2048,128]{1,0:T(8,128)(2,1)}, bf16[2048,128]{1,0:T(8,128)(2,1)}, bf16[2048,128]{1,0:T(8,128)(2,1)}) custom-call(bf16[1,128,2048]{2,1,0:T(8,128)(2,1)} %a_ref.1, bf16[1,128,2048]{2,1,0:T(8,128)(2,1)} %b_ref.1, bf16[1,128,2048]{2,1,0:T(8,128)(2,1)} %c_ref.1), custom_call_target="tpu_custom_call" | custom-call | tf_op jit(solution)/shard_map/gather_tokens/pallas_call | solution.py:262
  26.6 0.0 copy-done
  26.6 0.0 copy-start.1
  26.6 1.0 copy-done.1
  27.6 0.0 copy-start.2
  27.6 1.0 copy-done.2
  28.7 0.0 copy-start.3
  28.7 1.0 copy-done.3
  29.7 0.0 copy-start.4
  29.7 0.7 copy-done.4
  30.4 0.0 copy-start.5
  30.4 0.7 copy-done.5
  31.2 15.4 %transform.1 = (bf16[2048,128]{1,0:T(8,128)(2,1)S(1)}, bf16[2048,128]{1,0:T(8,128)(2,1)S(1)}, bf16[2048,128]{1,0:T(8,128)(2,1)S(1)}, f32[2048,128]{1,0:T(8,128)S(1)}) custom-call(bf16[2048,128]{1,0:T(8,128)(2,1)S(1)} %copy-done.1, bf16[2048,128]{1,0:T(8,128)(2,1)S(1)} %copy-done.3, bf16[2048,128]{1,0:T(8,128)(2,1)S(1)} %copy-done.2, ...), custom_call_target="tpu_custom_call" | custom-call | tf_op jit(solution)/shard_map/transform/pallas_call | solution.py:208
  46.5 73.7 %scatter_tokens.1 = (bf16[1,128,2048]{2,1,0:T(8,128)(2,1)S(1)}, bf16[1,128,2048]{2,1,0:T(8,128)(2,1)S(1)}, bf16[1,128,2048]{2,1,0:T(8,128)(2,1)S(1)}, f32[2048,128]{1,0:T(8,128)S(1)}) custom-call(bf16[2048,128]{1,0:T(8,128)(2,1)S(1)} %get-tuple-element.18.a_ref, bf16[2048,128]{1,0:T(8,128)(2,1)S(1)} %get-tuple-element.19.b_ref, ...), custom_call_target="tpu_custom_call" | custom-call | tf_op jit(solution)/shard_map/scatter_tokens/pallas_call | solution.py:390
  120.3 1.0 broadcast_multiply_fusion
  121.3 0.8 copy.15
  122.1 0.8 copy.16
  122.9 0.8 copy.17
Async XLA Ops:
  0.6 26.0 %copy-start = (f32[2048,128]{1,0:T(8,128)S(1)}, f32[2048,128]{1,0:T(8,128)}, u32[]{:S(2)}) copy-start(f32[2048,128]{1,0:T(8,128)} %h_ref.1) | copy-start | bytes 3145732
  26.6 1.0 copy-start.1
  27.6 1.0 copy-start.2
  28.7 1.0 copy-start.3
  29.7 0.7 copy-start.4
  30.4 0.7 copy-start.5

commit v2 on v0

v2 whole, which is shorter than its diff:
```python
import functools
import math

import jax
import jax.numpy as jnp
import ml_dtypes
import numpy as np
from jax import lax
from jax.experimental import pallas as pl
from jax.experimental.pallas import tpu as pltpu
from jax.sharding import PartitionSpec as P

MESH = pl.DeviceIdType.MESH
LANES = 128
SPLIT = 16
MIB = 1024 * 1024
UNROLL = 4


def two_pieces(table):
    high = table.astype(ml_dtypes.bfloat16)
    low = (table - high.astype(np.float64)).astype(ml_dtypes.bfloat16)
    return high, low


def build_tables(length):
    total = 2 * length
    rows = length // SPLIT
    time = np.arange(rows)[None, :] * SPLIT + np.arange(SPLIT)[:, None]
    angle = 2.0 * np.pi * (time[:, None, :] * np.arange(rows)[None, :, None] % total) / total
    real, imag = np.cos(angle), -np.sin(angle)
    real[:, 0, :] = 1.0
    imag[:, 0, :] = 1.0 - 2.0 * (np.arange(rows) % 2)
    high, low = two_pieces(np.concatenate([real, imag], 1))
    analysis = np.concatenate([high, low], 2)
    real, imag = np.cos(angle) * (2.0 / total), -np.sin(angle) * (2.0 / total)
    real[:, 0, :] = (np.arange(rows) % 2 == 0)[None, :]
    imag[:, 0, :] = (np.arange(rows) % 2 == 1)[None, :]
    high, low = two_pieces(np.concatenate([real, imag], 1).transpose(0, 2, 1))
    synthesis = np.concatenate([high, low], 1)
    edge = np.zeros((2 * SPLIT, 2 * SPLIT))
    back = np.zeros((2 * SPLIT, 2 * SPLIT))
    point = np.arange(SPLIT)
    folded = np.arange(2 * SPLIT)
    for m in range(SPLIT):
        turn = 2.0 * np.pi * m * point / (2 * SPLIT)
        start = SPLIT * (m % 2)
        edge[m, start : start + SPLIT] = np.cos(turn)
        full = 2.0 * np.pi * m * folded / (2 * SPLIT)
        if m:
            edge[SPLIT + m, start : start + SPLIT] = -np.sin(turn)
            back[:, m] = 2.0 * np.cos(full) / total
            back[:, SPLIT + m] = -2.0 * np.sin(full) / total
    edge[SPLIT, :SPLIT] = np.cos(np.pi * point)
    back[:, 0] = 1.0 / total
    back[:, SPLIT] = np.cos(np.pi * folded) / total
    return analysis, synthesis, edge.astype(np.float32), back.astype(np.float32)


def times(value, power, sign):
    re, im = value
    power = (power * sign) % 16
    if power == 0:
        return (re, im)
    if power == 4:
        return (-im, re)
    if power == 8:
        return (-re, -im)
    if power == 12:
        return (im, -re)
    c, s = math.cos(math.pi * power / 8), math.sin(math.pi * power / 8)
    if power % 4 == 2:
        size = math.sqrt(0.5)
        if power == 2:
            return ((re - im) * size, (re + im) * size)
        if power == 6:
            return ((re + im) * -size, (re - im) * size)
        if power == 10:
            return ((im - re) * size, (re + im) * -size)
        return ((re + im) * size, (im - re) * size)
    return (re * c - im * s, re * s + im * c)


def four(a, b, c, d, sign):
    sr, si = a[0] + c[0], a[1] + c[1]
    dr, di = a[0] - c[0], a[1] - c[1]
    tr, ti = b[0] + d[0], b[1] + d[1]
    er, ei = b[0] - d[0], b[1] - d[1]
    plus = (dr - ei, di + er)
    minus = (dr + ei, di - er)
    if sign < 0:
        plus, minus = minus, plus
    return ((sr + tr, si + ti), plus, (sr - tr, si - ti), minus)


def sixteen(points, sign):
    inner = [four(points[b], points[4 + b], points[8 + b], points[12 + b], sign) for b in range(4)]
    result = [None] * 16
    for c in range(4):
        column = [times(inner[b][c], b * c, sign) for b in range(4)]
        outer = four(*column, sign)
        for d in range(4):
            result[c + 4 * d] = outer[d]
    return result


def product(a, b, conjugate):
    if conjugate:
        return (a[0] * b[0] + a[1] * b[1], a[0] * b[1] - a[1] * b[0])
    return (a[0] * b[0] - a[1] * b[1], a[0] * b[1] + a[1] * b[0])


U, G, DU, H = range(4)
GRAD = 3
SUBS = 2


def fused_kernel(
    n, rings,
    u_ref, g_ref, du_ref, h_ref, analysis_ref, synthesis_ref, edge, back,
    ou_ref, og_ref, odu_ref, grad_ref,
    arrive, leave, impulse, analysis, synthesis, signal, spec, prod, rim, rim_spec, rim_mix, rim_out,
    part, right_box, left_box, pair_out, pair_in, total,
    table_sem, local_sem, in_send, in_recv, out_send, out_recv, sum_send, sum_recv, pair_sem, all_send, all_recv,
):
    me, dp = lax.axis_index("ctx"), lax.axis_index("dp")
    z, x = lax.div(dp, 2), lax.rem(dp, 2)
    up = {"dp": lax.rem(z + 1, rings) * 2 + x}
    down = {"dp": lax.rem(z + rings - 1, rings) * 2 + x}
    twin = {"dp": z * 2 + 1 - x}
    length = impulse.shape[0]
    rows = length // SPLIT
    tokens = length // n
    far, near = rings // 2, rings // 2 - 1
    sub = rows // SUBS
    mine = pl.ds(pl.multiple_of(me * tokens, tokens), tokens)
    own = pl.ds(pl.multiple_of(me * LANES, LANES), LANES)

    tables = [
        pltpu.make_async_copy(src, dst, table_sem.at[i])
        for i, (src, dst) in enumerate(((h_ref, impulse), (analysis_ref, analysis), (synthesis_ref, synthesis)))
    ]
    for copy in tables:
        copy.start()
    barrier = pltpu.get_barrier_semaphore()
    for step in range(1, n):
        pl.semaphore_signal(
            barrier, inc=1, device_id={"ctx": lax.rem(me + step, n)}, device_id_type=MESH
        )
    for device in (up, down, twin):
        pl.semaphore_signal(barrier, inc=1, device_id=device, device_id_type=MESH)
    pl.semaphore_wait(barrier, n + 2)

    remote, sent, locals_ = {}, [], {}

    def send_in(s):
        src = (u_ref, g_ref, du_ref)[s]
        remote[s] = []
        for step in range(1, n):
            other = lax.rem(me + step, n)
            copy = pltpu.make_async_remote_copy(
                src_ref=src.at[0, :, pl.ds(pl.multiple_of(other * LANES, LANES), LANES)],
                dst_ref=arrive.at[s, mine, :],
                send_sem=in_send.at[s, step], recv_sem=in_recv.at[s, step],
                device_id={"ctx": other}, device_id_type=MESH,
            )
            copy.start()
            remote[s].append(copy)
        locals_[s] = pltpu.make_async_copy(src.at[0, :, own], arrive.at[s, mine, :], local_sem.at[s])
        locals_[s].start()

    def receive(s):
        for copy in remote[s]:
            copy.wait_recv()
        locals_[s].wait()
        sent.extend(remote[s])

    finished = []

    def send_out(o):
        dst = (ou_ref, og_ref, odu_ref)[o]
        for step in range(1, n):
            other = lax.rem(me + step, n)
            copy = pltpu.make_async_remote_copy(
                src_ref=leave.at[o, pl.ds(pl.multiple_of(other * tokens, tokens), tokens), :],
                dst_ref=dst.at[0, :, own],
                send_sem=out_send.at[o, step], recv_sem=out_recv.at[o, step],
                device_id={"ctx": other}, device_id_type=MESH,
            )
            copy.start()
            finished.append(copy)
        copy = pltpu.make_async_copy(leave.at[o, mine, :], dst.at[0, :, own], local_sem.at[3 + o])
        copy.start()
        finished.append(copy)

    def analyse(s, slots):
        def body(q, carry):
            pieces = [signal[i, pl.ds(q, rows, stride=SPLIT), :].astype(jnp.bfloat16) for i in slots]
            block = jnp.concatenate(pieces, 1) if len(slots) > 1 else pieces[0]
            block = jnp.concatenate([block, block], 0)
            out = jnp.dot(analysis[q], block, preferred_element_type=jnp.float32)
            if len(slots) > 1:
                out = out[:, :LANES] + out[:, LANES:]
            spec[s, q] = out
            rim[pl.ds(q, 1), :] = out[0:1]
            rim[pl.ds(SPLIT + q, 1), :] = out[rows : rows + 1]
            return carry

        lax.fori_loop(0, SPLIT, body, 0, unroll=UNROLL)
        rim_spec[s] = jnp.dot(
            edge[...], rim[...], precision=lax.Precision.HIGHEST, preferred_element_type=jnp.float32
        )

    def mix(o, a, b, conjugate, turned, kept):
        left, right = (rim_spec[a, :SPLIT], rim_spec[a, SPLIT:]), (rim_spec[b, :SPLIT], rim_spec[b, SPLIT:])
        re, im = product(left, right, conjugate)
        first = lax.broadcasted_iota(jnp.int32, (SPLIT, LANES), 0) == 0
        rim_mix[:SPLIT] = jnp.where(first, left[0] * right[0], re)
        rim_mix[SPLIT:] = jnp.where(first, left[1] * right[1], im)
        rim_out[o] = jnp.dot(
            back[...], rim_mix[...], precision=lax.Precision.HIGHEST, preferred_element_type=jnp.float32
        )

        def body(tile, carry):
            upper = pl.ds(pl.multiple_of(tile * 8, 8), 8)
            lower = pl.ds(pl.multiple_of(rows + tile * 8, 8), 8)
            points = [(spec[b, j, upper, :], spec[b, j, lower, :]) for j in range(SPLIT)]
            if not turned:
                points = sixteen(points, -1)
                if kept:
                    for j in range(SPLIT):
                        spec[b, j, upper, :] = points[j][0]
                        spec[b, j, lower, :] = points[j][1]
            points = [
                product((spec[a, j, upper, :], spec[a, j, lower, :]), points[j], conjugate)
                for j in range(SPLIT)
            ]
            points = sixteen(points, 1)
            for q in range(SPLIT):
                prod[o, q, upper, :] = points[q][0]
                prod[o, q, lower, :] = points[q][1]
            return carry

        lax.fori_loop(0, rows // 8, body, 0)

    def turn(s):
        def body(tile, carry):
            upper = pl.ds(pl.multiple_of(tile * 8, 8), 8)
            lower = pl.ds(pl.multiple_of(rows + tile * 8, 8), 8)
            points = sixteen([(spec[s, q, upper, :], spec[s, q, lower, :]) for q in range(SPLIT)], -1)
            for j in range(SPLIT):
                spec[s, j, upper, :] = points[j][0]
                spec[s, j, lower, :] = points[j][1]
            return carry

        lax.fori_loop(0, rows // 8, body, 0)

    def residue(o, q):
        prod[o, q, 0:1, :] = rim_out[o, pl.ds(q, 1), :]
        prod[o, q, rows : rows + 1, :] = rim_out[o, pl.ds(SPLIT + q, 1), :]
        block = prod[o, q]
        top = block.astype(jnp.bfloat16)
        rest = (block - top.astype(jnp.float32)).astype(jnp.bfloat16)
        both = jnp.dot(synthesis[q], top, preferred_element_type=jnp.float32)
        more = jnp.dot(synthesis[q, :rows], rest, preferred_element_type=jnp.float32)
        return both[:rows] + (both[rows:] + more)

    def finish(o):
        def body(q, carry):
            signal[o, pl.ds(q, rows, stride=SPLIT), :] = residue(o, q)
            return carry

        lax.fori_loop(0, SPLIT, body, 0, unroll=UNROLL)
        leave[o] = signal[o].astype(jnp.bfloat16)

    def load(s):
        signal[s] = arrive[s].astype(jnp.float32)

    def place(index):
        return lax.rem(index + 2 * rings, rings)

    started = []

    def hop(src, dst, sends, recvs, device):
        copy = pltpu.make_async_remote_copy(
            src_ref=src, dst_ref=dst, send_sem=sends, recv_sem=recvs, device_id=device, device_id_type=MESH
        )
        copy.start()
        started.append(copy)
        return copy

    cuts = [pl.ds(c * sub, sub) for c in range(SUBS)]

    send_in(U)
    send_in(G)
    tables[0].wait()
    high = impulse[...].astype(jnp.bfloat16).astype(jnp.float32)
    signal[0] = high
    signal[1] = impulse[...] - high
    tables[1].wait()
    analyse(H, (0, 1))
    turn(H)
    receive(U)
    load(U)
    analyse(U, (U,))
    mix(U, H, U, False, False, True)
    tables[2].wait()
    finish(U)
    receive(G)
    load(G)
    analyse(G, (G,))
    mix(GRAD, U, G, True, False, True)

    def chunk(q):
        part[q] = residue(GRAD, q)

    chunk(place(z + far))
    chunk(place(z - near))
    right = [
        hop(part.at[place(z + far), c], right_box.at[0, c], sum_send.at[0, 0, i], sum_recv.at[0, 0, i], up)
        for i, c in enumerate(cuts)
    ]
    left = [
        hop(part.at[place(z - near), c], left_box.at[0, c], sum_send.at[1, 0, i], sum_recv.at[1, 0, i], down)
        for i, c in enumerate(cuts)
    ]

    def others(step, carry):
        chunk(place(z - near + step))
        return carry

    lax.fori_loop(1, rings - 1, others, 0, unroll=2)
    send_out(U)
    send_in(DU)

    def last_product():
        receive(DU)
        load(DU)
        analyse(DU, (DU,))

    work = {
        1: lambda: mix(G, H, G, True, True, False),
        2: lambda: (finish(G), send_out(G)),
        4: last_product,
        5: lambda: mix(DU, H, DU, False, False, False),
        6: lambda: (finish(DU), send_out(DU)),
    }
    for step in range(1, far):
        for i, c in enumerate(cuts):
            right[i].wait_recv()
            right_box[step - 1, c] += part[place(z + far - step), c]
            right[i] = hop(
                right_box.at[step - 1, c], right_box.at[step, c],
                sum_send.at[0, step, i], sum_recv.at[0, step, i], up,
            )
            if step < near:
                left[i].wait_recv()
                left_box[step - 1, c] += part[place(z - near + step), c]
                left[i] = hop(
                    left_box.at[step - 1, c], left_box.at[step, c],
                    sum_send.at[1, step, i], sum_recv.at[1, step, i], down,
                )
        if step in work:
            work[step]()
    pair = []
    for i, c in enumerate(cuts):
        left[i].wait_recv()
        right[i].wait_recv()
        pair_out[c] = part[place(z), c] + (right_box[far - 1, c] + left_box[near - 1, c])
        pair.append(hop(pair_out.at[c], pair_in.at[c], pair_sem.at[0, i], pair_sem.at[1, i], twin))
    for step in range(far):
        for i, c in enumerate(cuts):
            if step:
                right[i].wait_recv()
            else:
                pair[i].wait_recv()
                total[z, c] = pair_out[c] + pair_in[c]
            here = total.at[place(z - step), c]
            right[i] = hop(here, here, all_send.at[0, step, i], all_recv.at[0, step, i], up)
            if step < near:
                if step:
                    left[i].wait_recv()
                here = total.at[place(z + step), c]
                left[i] = hop(here, here, all_send.at[1, step, i], all_recv.at[1, step, i], down)
    for i in range(SUBS):
        right[i].wait_recv()
        left[i].wait_recv()
    for q in range(SPLIT):
        grad_ref[pl.ds(q, rows, stride=SPLIT), :] = total[q]
    for copy in started + sent:
        copy.wait_send()
    for copy in finished:
        copy.wait()


def fused(u, g, du, h, tables):
    n = lax.axis_size("ctx")
    rings = lax.axis_size("dp") // 2
    length, width = h.shape
    rows = length // SPLIT
    far = rings // 2
    anywhere = pl.BlockSpec(memory_space=pl.ANY)
    whole = pl.BlockSpec(memory_space=pltpu.VMEM)
    shape = jax.ShapeDtypeStruct((1, length // n, n * width), jnp.bfloat16)
    sem = pltpu.SemaphoreType.DMA

    def space(*sizes, kind=jnp.float32):
        return pltpu.VMEM(sizes, kind)

    half = jnp.bfloat16
    return pl.pallas_call(
        functools.partial(fused_kernel, n, rings),
        out_shape=(shape,) * 3 + (jax.ShapeDtypeStruct((length, width), jnp.float32),),
        in_specs=[anywhere] * 6 + [whole] * 2,
        out_specs=(anywhere,) * 3 + (whole,),
        scratch_shapes=[
            space(3, length, width, kind=half),
            space(3, length, width, kind=half),
            space(length, width),
            space(*tables[0].shape, kind=half),
            space(*tables[1].shape, kind=half),
            space(3, length, width),
            space(4, SPLIT, 2 * rows, width),
            space(4, SPLIT, 2 * rows, width),
            space(2 * SPLIT, width),
            space(4, 2 * SPLIT, width),
            space(2 * SPLIT, width),
            space(4, 2 * SPLIT, width),
            space(rings, rows, width),
            space(far, rows, width),
            space(far, rows, width),
            space(rows, width),
            space(rows, width),
            space(rings, rows, width),
            sem((3,)), sem((6,)),
            sem((3, n)), sem((3, n)), sem((3, n)), sem((3, n)),
            sem((2, far, SUBS)), sem((2, far, SUBS)), sem((2, SUBS)),
            sem((2, far, SUBS)), sem((2, far, SUBS)),
        ],
        compiler_params=pltpu.CompilerParams(
            collective_id=0, has_side_effects=True, vmem_limit_bytes=48 * MIB
        ),
        name="hyena",
    )(u, g, du, h, *tables)


def local(primal, tangent, cotangent, impulse):
    length = impulse.shape[0]
    tables = [jnp.asarray(t) for t in build_tables(length)]
    back_u, back_g, back_du, summed = fused(primal, cotangent, tangent, impulse, tables)
    scale = 1.0 / math.sqrt(lax.axis_size("dp") * length)
    return (back_u, back_du, back_g, summed * scale)


def solution(mesh):
    placed = (P("dp", "ctx", None), P("dp", "ctx", None), P("dp", "ctx", None), P(None, "ctx"))
    return jax.shard_map(
        local,
        mesh=mesh,
        in_specs=placed,
        out_specs=(
            P("dp", "ctx", None),
            P("dp", "ctx", None),
            P("dp", "ctx", None),
            P(None, "ctx"),
        ),
        check_vma=False,
    )
```

time: 508 us -> 104 us (0.20)
  waiting for transfers between devices: 202 us -> 0 us
  Pallas kernels: 0 us -> 93.7 us
  other arithmetic: 88 us -> 1.04 us
  matrix products: 78.7 us -> 0 us
  local copies, waits for them, and re-layouts: 72.6 us -> 8.15 us
  starting transfers between devices: 46.5 us -> 0 us
  between operations: 14.7 us -> 0.65 us
    psum x1 -> x0, waiting for transfers between devices: 196 us -> none  [local(): summed = lax.psum(partial_grad, 'dp')]
    pallas_call x0 -> x1, Pallas kernels: none -> 93.7 us  [fused(): pl.pallas_call(functools.partial(fused_kernel, n, rings), out_shape=(shap...]
    dot_general x12 -> x0, matrix products: 78.7 us -> none  [the longest x4 29.6 us: forward_spectrum(): jnp.einsum('ajbq,bkqc->akjc', second, middle, precision=lax.Precision.HIG...]
    unnamed x6 -> x0, other arithmetic: 71.6 us -> none
    all_to_all x6 -> x0, starting transfers between devices: 46.5 us -> none  [the longest x1 10.1 us: local(): lax.all_to_all(tangent, 'ctx', split_axis=2, concat_axis=1, tiled=True)]
    convert_element_type x6 -> x0, local copies, waits for them, and re-layouts: 31 us -> none  [the longest x1 8.92 us: local(): result_u = forward_out[0:1].astype(jnp.bfloat16)]
    unnamed x45 -> x15, local copies, waits for them, and re-layouts: 32.5 us -> 8.15 us
    all_to_all x6 -> x0, waiting for transfers between devices: 6.2 us -> none  [the longest x1 6.18 us: local(): lax.all_to_all(result_g, 'ctx', split_axis=1, concat_axis=2, tiled=True)]
  transfers between devices with their start and end apart: 7 -> 0, of which waited for: 2 -> 0; matrix products, arithmetic and copies ran while one was open for 44% -> 0% of each run, Pallas kernels for 0% -> 0%
where the time goes in v2:
time: 104 us
  Pallas kernels  93.7 us (90%)
  local copies, waits for them, and re-layouts  8.15 us (8%)
  other arithmetic  1.04 us (1%)
    pallas_call x1, Pallas kernels, fused(): pl.pallas_call(functools.partial(fused_kernel, n, rings), out_shape=(shap...  93.7 us
    unnamed x15, local copies, waits for them, and re-layouts  8.15 us

profile of v2, /device:TPU:24, one launch (start us, length us, event | category | flops | bytes accessed | tf_op | source)
XLA Modules:
  0.0 103.5 jit_solution(6347902995059098122)
XLA Ops:
  0.6 0.0 copy-start
  0.6 1.2 %copy-done = f32[2048,128]{1,0:T(8,128)S(1)} copy-done((f32[2048,128]{1,0:T(8,128)S(1)}, f32[2048,128]{1,0:T(8,128)}, u32[]{:S(2)}) %copy-start) | copy-done | bytes 1048600
  1.9 0.0 copy-start.1
  1.9 1.0 %copy-done.1 = bf16[1,128,2048]{2,1,0:T(8,128)(2,1)S(1)} copy-done((bf16[1,128,2048]{2,1,0:T(8,128)(2,1)S(1)}, bf16[1,128,2048]{2,1,0:T(8,128)(2,1)}, u32[]{:S(2)}) %copy-start.1) | copy-done | bytes 524312
  2.9 0.0 copy-start.2
  2.9 1.0 %copy-done.2 = bf16[1,128,2048]{2,1,0:T(8,128)(2,1)S(1)} copy-done((bf16[1,128,2048]{2,1,0:T(8,128)(2,1)S(1)}, bf16[1,128,2048]{2,1,0:T(8,128)(2,1)}, u32[]{:S(2)}) %copy-start.2) | copy-done | bytes 524312
  3.9 0.0 copy-start.3
  3.9 1.0 %copy-done.3 = bf16[1,128,2048]{2,1,0:T(8,128)(2,1)S(1)} copy-done((bf16[1,128,2048]{2,1,0:T(8,128)(2,1)S(1)}, bf16[1,128,2048]{2,1,0:T(8,128)(2,1)}, u32[]{:S(2)}) %copy-start.3) | copy-done | bytes 524312
  5.0 0.0 copy-start.4
  5.0 0.7 copy-done.4
  5.7 0.0 copy-start.5
  5.7 0.7 copy-done.5
  6.4 93.7 %hyena.1 = (bf16[1,128,2048]{2,1,0:T(8,128)(2,1)S(1)}, bf16[1,128,2048]{2,1,0:T(8,128)(2,1)S(1)}, bf16[1,128,2048]{2,1,0:T(8,128)(2,1)S(1)}, f32[2048,128]{1,0:T(8,128)S(1)}) custom-call(bf16[1,128,2048]{2,1,0:T(8,128)(2,1)S(1)} %copy-done.1, bf16[1,128,2048]{2,1,0:T(8,128)(2,1)S(1)} %copy-done.2, bf16[1,128,2048]{2,1,0:T(8,128)(2,1)S(1)} %copy-done.3, ...), custom_call_target="tpu_custom_call" | custom-call | tf_op jit(solution)/shard_map/hyena/pallas_call | solution.py:411
  100.1 1.0 %broadcast_multiply_fusion = f32[2048,128]{1,0:T(8,128)} fusion(f32[2048,128]{1,0:T(8,128)S(1)} %get-tuple-element.11), kind=kLoop, calls=%fused_computation | loop fusion | flops 262144 | bytes 2097152 | tf_op jit(solution)/shard_map/mul | solution.py:452
  101.1 0.8 copy.15
  101.9 0.8 copy.16
  102.7 0.8 copy.17
Async XLA Ops:
  0.6 1.2 %copy-start = (f32[2048,128]{1,0:T(8,128)S(1)}, f32[2048,128]{1,0:T(8,128)}, u32[]{:S(2)}) copy-start(f32[2048,128]{1,0:T(8,128)} %h_ref.1) | copy-start | bytes 3145732
  1.9 1.0 %copy-start.1 = (bf16[1,128,2048]{2,1,0:T(8,128)(2,1)S(1)}, bf16[1,128,2048]{2,1,0:T(8,128)(2,1)}, u32[]{:S(2)}) copy-start(bf16[1,128,2048]{2,1,0:T(8,128)(2,1)} %u_ref.1) | copy-start | bytes 1572868
  2.9 1.0 %copy-start.2 = (bf16[1,128,2048]{2,1,0:T(8,128)(2,1)S(1)}, bf16[1,128,2048]{2,1,0:T(8,128)(2,1)}, u32[]{:S(2)}) copy-start(bf16[1,128,2048]{2,1,0:T(8,128)(2,1)} %g_ref.1) | copy-start | bytes 1572868
  3.9 1.0 %copy-start.3 = (bf16[1,128,2048]{2,1,0:T(8,128)(2,1)S(1)}, bf16[1,128,2048]{2,1,0:T(8,128)(2,1)}, u32[]{:S(2)}) copy-start(bf16[1,128,2048]{2,1,0:T(8,128)(2,1)} %du_ref.1) | copy-start | bytes 1572868
  5.0 0.7 copy-start.4
  5.7 0.7 copy-start.5

commit v3 on v2

--- a/solution.py
+++ b/solution.py
@@ -14,7 +14,7 @@
 LANES = 128
 SPLIT = 16
 MIB = 1024 * 1024
-UNROLL = 4
+UNROLL = 16
 
 
 def two_pieces(table):
@@ -116,22 +116,27 @@
 
 
 def fused_kernel(
-    n, rings,
+    n, rings, scale,
     u_ref, g_ref, du_ref, h_ref, analysis_ref, synthesis_ref, edge, back,
     ou_ref, og_ref, odu_ref, grad_ref,
     arrive, leave, impulse, analysis, synthesis, signal, spec, prod, rim, rim_spec, rim_mix, rim_out,
-    part, right_box, left_box, pair_out, pair_in, total,
-    table_sem, local_sem, in_send, in_recv, out_send, out_recv, sum_send, sum_recv, pair_sem, all_send, all_recv,
+    part, right_box, left_box, right_leaf, left_leaf, landing, total,
+    table_sem, local_sem, in_send, in_recv, out_send, out_recv, sum_send, sum_recv, leaf_send, leaf_recv, land_send, land_recv,
+    all_send, all_recv, near_send, near_recv, twin_send, twin_recv,
 ):
     me, dp = lax.axis_index("ctx"), lax.axis_index("dp")
     z, x = lax.div(dp, 2), lax.rem(dp, 2)
-    up = {"dp": lax.rem(z + 1, rings) * 2 + x}
-    down = {"dp": lax.rem(z + rings - 1, rings) * 2 + x}
+    up, up_two, down, down_two = (
+        {"dp": lax.rem(z + move, rings) * 2 + x} for move in (1, 2, rings - 1, rings - 2)
+    )
     twin = {"dp": z * 2 + 1 - x}
+    around = [
+        {"dp": lax.rem(z + move, rings) * 2 + 1 - x} for move in (1, 2, rings - 1, rings - 2)
+    ]
     length = impulse.shape[0]
     rows = length // SPLIT
     tokens = length // n
-    far, near = rings // 2, rings // 2 - 1
+    steps = rings // 4
     sub = rows // SUBS
     mine = pl.ds(pl.multiple_of(me * tokens, tokens), tokens)
     own = pl.ds(pl.multiple_of(me * LANES, LANES), LANES)
@@ -147,9 +152,9 @@
         pl.semaphore_signal(
             barrier, inc=1, device_id={"ctx": lax.rem(me + step, n)}, device_id_type=MESH
         )
-    for device in (up, down, twin):
+    for device in (up, up_two, down, down_two, twin, *around):
         pl.semaphore_signal(barrier, inc=1, device_id=device, device_id_type=MESH)
-    pl.semaphore_wait(barrier, n + 2)
+    pl.semaphore_wait(barrier, n + 8)
 
     remote, sent, locals_ = {}, [], {}
 
@@ -303,102 +308,172 @@
     receive(U)
     load(U)
     analyse(U, (U,))
-    mix(U, H, U, False, False, True)
-    tables[2].wait()
-    finish(U)
+    turn(U)
     receive(G)
     load(G)
     analyse(G, (G,))
     mix(GRAD, U, G, True, False, True)
+    tables[2].wait()
 
     def chunk(q):
         part[q] = residue(GRAD, q)
 
-    chunk(place(z + far))
-    chunk(place(z - near))
-    right = [
-        hop(part.at[place(z + far), c], right_box.at[0, c], sum_send.at[0, 0, i], sum_recv.at[0, 0, i], up)
-        for i, c in enumerate(cuts)
-    ]
-    left = [
-        hop(part.at[place(z - near), c], left_box.at[0, c], sum_send.at[1, 0, i], sum_recv.at[1, 0, i], down)
-        for i, c in enumerate(cuts)
-    ]
+    def leaf(side, i):
+        src, dst, device = (
+            (part.at[place(z + 2 * steps - 1 - 2 * i)], right_leaf.at[i], up),
+            (part.at[place(z - 2 * steps + 1 + 2 * i)], left_leaf.at[i], down),
+        )[side]
+        return hop(src, dst, leaf_send.at[side, i], leaf_recv.at[side, i], device)
+
+    def chain(side, step, source):
+        box, device = ((right_box, up_two), (left_box, down_two))[side]
+        return [
+            hop(source(c), box.at[step, c], sum_send.at[side, step, i], sum_recv.at[side, step, i], device)
+            for i, c in enumerate(cuts)
+        ]
+
+    chunk(place(z + 2 * steps))
+    right = chain(0, 0, lambda c: part.at[place(z + 2 * steps), c])
+    chunk(place(z - 2 * steps + 1))
+    left_leaves = [leaf(1, 0)]
+    chunk(place(z + 2 * steps - 1))
+    right_leaves = [leaf(0, 0)]
 
     def others(step, carry):
-        chunk(place(z - near + step))
+        chunk(place(z - 2 * steps + 1 + step))
         return carry
 
-    lax.fori_loop(1, rings - 1, others, 0, unroll=2)
-    send_out(U)
-    send_in(DU)
-
-    def last_product():
-        receive(DU)
-        load(DU)
-        analyse(DU, (DU,))
-
-    work = {
-        1: lambda: mix(G, H, G, True, True, False),
-        2: lambda: (finish(G), send_out(G)),
-        4: last_product,
-        5: lambda: mix(DU, H, DU, False, False, False),
-        6: lambda: (finish(DU), send_out(DU)),
-    }
-    for step in range(1, far):
+    lax.fori_loop(1, rings - 2, others, 0, unroll=rings - 3)
+    for i in range(1, steps - 1):
+        left_leaves.append(leaf(1, i))
+        right_leaves.append(leaf(0, i))
+
+    def sum_left(step, left):
+        left_leaves[step].wait_recv()
+        q = place(z - 2 * steps + 2 + 2 * step)
+        if step == 0:
+            for c in cuts:
+                left_leaf[0, c] += part[q, c]
+            return chain(1, 0, lambda c: left_leaf.at[0, c])
+        for i, c in enumerate(cuts):
+            left[i].wait_recv()
+            left_box[step - 1, c] += part[q, c] + left_leaf[step, c]
+        if step == steps - 2:
+            return land(1, rings - 2, lambda c: left_box.at[step - 1, c])
+        return chain(1, step, lambda c: left_box.at[step - 1, c])
+
+    def sum_right(step, right):
+        right_leaves[step - 1].wait_recv()
+        q = place(z + 2 * steps - 2 * step)
         for i, c in enumerate(cuts):
             right[i].wait_recv()
-            right_box[step - 1, c] += part[place(z + far - step), c]
-            right[i] = hop(
-                right_box.at[step - 1, c], right_box.at[step, c],
-                sum_send.at[0, step, i], sum_recv.at[0, step, i], up,
+            right_box[step - 1, c] += part[q, c] + right_leaf[step - 1, c]
+        if step == steps - 1:
+            return land(0, 2, lambda c: right_box.at[step - 1, c])
+        return chain(0, step, lambda c: right_box.at[step - 1, c])
+
+    half = rows // 2
+    kept = pl.ds(pl.multiple_of(x * half, half), half)
+    given = pl.ds(pl.multiple_of((1 - x) * half, half), half)
+
+    def land(kind, move, source):
+        for rail in range(2):
+            device = {"dp": lax.rem(z + move, rings) * 2 + rail}
+            hop(
+                source(pl.ds(rail * half, half)), landing.at[kind, x],
+                land_send.at[kind, rail], land_recv.at[kind, x], device,
             )
-            if step < near:
-                left[i].wait_recv()
-                left_box[step - 1, c] += part[place(z - near + step), c]
-                left[i] = hop(
-                    left_box.at[step - 1, c], left_box.at[step, c],
-                    sum_send.at[1, step, i], sum_recv.at[1, step, i], down,
-                )
-        if step in work:
-            work[step]()
-    pair = []
-    for i, c in enumerate(cuts):
-        left[i].wait_recv()
-        right[i].wait_recv()
-        pair_out[c] = part[place(z), c] + (right_box[far - 1, c] + left_box[near - 1, c])
-        pair.append(hop(pair_out.at[c], pair_in.at[c], pair_sem.at[0, i], pair_sem.at[1, i], twin))
-    for step in range(far):
-        for i, c in enumerate(cuts):
-            if step:
-                right[i].wait_recv()
-            else:
-                pair[i].wait_recv()
-                total[z, c] = pair_out[c] + pair_in[c]
-            here = total.at[place(z - step), c]
-            right[i] = hop(here, here, all_send.at[0, step, i], all_recv.at[0, step, i], up)
-            if step < near:
-                if step:
-                    left[i].wait_recv()
-                here = total.at[place(z + step), c]
-                left[i] = hop(here, here, all_send.at[1, step, i], all_recv.at[1, step, i], down)
-    for i in range(SUBS):
-        right[i].wait_recv()
-        left[i].wait_recv()
+
+    def landed(kind, rail):
+        pltpu.make_async_remote_copy(
+            src_ref=landing.at[kind, rail], dst_ref=landing.at[kind, rail],
+            send_sem=land_send.at[kind, rail], recv_sem=land_recv.at[kind, rail],
+            device_id=twin, device_id_type=MESH,
+        ).wait_recv()
+
+    gift = hop(part.at[z, given], landing.at[4, 0], land_send.at[4, 0], land_recv.at[4, 0], twin)
+    land(2, 1, lambda c: part.at[place(z + 1), c])
+    land(3, rings - 1, lambda c: part.at[place(z - 1), c])
+    send_in(DU)
+    left = sum_left(0, None)
+    right = sum_right(1, right)
+    mix(U, H, U, False, True, False)
+    finish(U)
+    send_out(U)
+    left = sum_left(1, left)
+    right = sum_right(2, right)
+    mix(G, H, G, True, True, False)
+    finish(G)
+    send_out(G)
+    sum_left(2, left)
+    sum_right(3, right)
+    receive(DU)
+    load(DU)
+    analyse(DU, (DU,))
+    mix(DU, H, DU, False, False, False)
+    gift.wait_recv()
+    mine_sum = part[z, kept] + landing[4, 0]
+    for kind in (2, 3, 1, 0):
+        for rail in range(2):
+            landed(kind, rail)
+        mine_sum = mine_sum + (landing[kind, 0] + landing[kind, 1])
+    total[z, kept] = mine_sum
+
+    shared = []
+
+    def spread(side, step, last_chain):
+        index = place(z - 2 * step) if side == 0 else place(z + 2 * step)
+        two, one = ((up_two, up), (down_two, down))[side]
+        here = total.at[index, kept]
+        first = None
+        if not last_chain:
+            first = hop(here, here, all_send.at[side, step], all_recv.at[side, step], two)
+        second = hop(here, here, near_send.at[side, step], near_recv.at[side, step], one)
+        if side == 0 or step:
+            share(index)
+        return first, second
+
+    def share(index):
+        here = total.at[index, kept]
+        i = len(shared)
+        shared.append(hop(here, here, twin_send.at[i], twin_recv.at[i], twin))
+
+    right, right_near = spread(0, 0, False)
+    left, left_near = spread(1, 0, False)
+    finish(DU)
+    send_out(DU)
+    for step in range(1, steps):
+        behind = (right_near, left_near)
+        right.wait_recv()
+        right, right_near = spread(0, step, False)
+        left.wait_recv()
+        left, left_near = spread(1, step, step == steps - 1)
+        behind[0].wait_recv()
+        share(place(z - 2 * step + 1))
+        behind[1].wait_recv()
+        share(place(z + 2 * step - 1))
+    right.wait_recv()
+    share(place(z - 2 * steps))
+    right_near.wait_recv()
+    share(place(z - 2 * steps + 1))
+    left_near.wait_recv()
+    share(place(z + 2 * steps - 1))
+    for copy in shared:
+        copy.wait_recv()
     for q in range(SPLIT):
-        grad_ref[pl.ds(q, rows, stride=SPLIT), :] = total[q]
+        grad_ref[pl.ds(q, rows, stride=SPLIT), :] = total[q] * scale
     for copy in started + sent:
         copy.wait_send()
     for copy in finished:
         copy.wait()
 
 
-def fused(u, g, du, h, tables):
+def fused(u, g, du, h, tables, scale):
     n = lax.axis_size("ctx")
     rings = lax.axis_size("dp") // 2
     length, width = h.shape
     rows = length // SPLIT
-    far = rings // 2
+    steps = rings // 4
     anywhere = pl.BlockSpec(memory_space=pl.ANY)
     whole = pl.BlockSpec(memory_space=pltpu.VMEM)
     shape = jax.ShapeDtypeStruct((1, length // n, n * width), jnp.bfloat16)
@@ -409,7 +484,7 @@
 
     half = jnp.bfloat16
     return pl.pallas_call(
-        functools.partial(fused_kernel, n, rings),
+        functools.partial(fused_kernel, n, rings, scale),
         out_shape=(shape,) * 3 + (jax.ShapeDtypeStruct((length, width), jnp.float32),),
         in_specs=[anywhere] * 6 + [whole] * 2,
         out_specs=(anywhere,) * 3 + (whole,),
@@ -427,29 +502,59 @@
             space(2 * SPLIT, width),
             space(4, 2 * SPLIT, width),
             space(rings, rows, width),
-            space(far, rows, width),
-            space(far, rows, width),
-            space(rows, width),
-            space(rows, width),
+            space(steps - 1, rows, width),
+            space(steps - 1, rows, width),
+            space(steps - 1, rows, width),
+            space(steps - 1, rows, width),
+            space(5, 2, rows // 2, width),
             space(rings, rows, width),
             sem((3,)), sem((6,)),
             sem((3, n)), sem((3, n)), sem((3, n)), sem((3, n)),
-            sem((2, far, SUBS)), sem((2, far, SUBS)), sem((2, SUBS)),
-            sem((2, far, SUBS)), sem((2, far, SUBS)),
+            sem((2, steps, SUBS)), sem((2, steps, SUBS)), sem((2, steps)), sem((2, steps)), sem((5, 2)), sem((5, 2)),
+            sem((2, steps)), sem((2, steps)), sem((2, steps)), sem((2, steps)), sem((rings,)), sem((rings,)),
         ],
         compiler_params=pltpu.CompilerParams(
-            collective_id=0, has_side_effects=True, vmem_limit_bytes=48 * MIB
+            collective_id=0, has_side_effects=True, vmem_limit_bytes=60 * MIB
         ),
         name="hyena",
     )(u, g, du, h, *tables)
 
 
+def copy_kernel(count, *refs):
+    sources, targets, staged = refs[:count], refs[count : 2 * count], refs[2 * count : 3 * count]
+    read_sem, write_sem = refs[3 * count :]
+    reads = [pltpu.make_async_copy(sources[i], staged[i], read_sem.at[i]) for i in range(count)]
+    writes = [pltpu.make_async_copy(staged[i], targets[i], write_sem.at[i]) for i in range(count)]
+    for copy in reads:
+        copy.start()
+    for i in range(count):
+        reads[i].wait()
+        writes[i].start()
+    for copy in writes:
+        copy.wait()
+
+
+def copied(*arrays):
+    count = len(arrays)
+    anywhere = pl.BlockSpec(memory_space=pl.ANY)
+    return pl.pallas_call(
+        functools.partial(copy_kernel, count),
+        out_shape=tuple(jax.ShapeDtypeStruct(a.shape, a.dtype) for a in arrays),
+        in_specs=[anywhere] * count,
+        out_specs=(anywhere,) * count,
+        scratch_shapes=[pltpu.VMEM(a.shape, a.dtype) for a in arrays]
+        + [pltpu.SemaphoreType.DMA((count,)), pltpu.SemaphoreType.DMA((count,))],
+        compiler_params=pltpu.CompilerParams(vmem_limit_bytes=60 * MIB),
+        name="results",
+    )(*arrays)
+
+
 def local(primal, tangent, cotangent, impulse):
     length = impulse.shape[0]
     tables = [jnp.asarray(t) for t in build_tables(length)]
-    back_u, back_g, back_du, summed = fused(primal, cotangent, tangent, impulse, tables)
     scale = 1.0 / math.sqrt(lax.axis_size("dp") * length)
-    return (back_u, back_du, back_g, summed * scale)
+    back_u, back_g, back_du, summed = copied(*fused(primal, cotangent, tangent, impulse, tables, scale))
+    return (back_u, back_du, back_g, summed)
 
 
 def solution(mesh):

time: 104 us -> 83.2 us (0.80)
  Pallas kernels: 93.7 us -> 81.5 us
  local copies, waits for them, and re-layouts: 8.15 us -> 0 us
  other arithmetic: 1.04 us -> 0 us
    pallas_call x1 -> x2, Pallas kernels: 93.7 us -> 81.5 us  [the longest x1 78.8 us: fused(): pl.pallas_call(functools.partial(fused_kernel, n, rings, scale), out_shap...]
    unnamed x15 -> x0, local copies, waits for them, and re-layouts: 8.15 us -> none
where the time goes in v3:
time: 83.2 us; the launch traced here: 82.2 us
  Pallas kernels  81.5 us (98%)
    pallas_call x1, Pallas kernels, fused(): pl.pallas_call(functools.partial(fused_kernel, n, rings, scale), out_shap...  78.8 us
    pallas_call x1, Pallas kernels, copied(): pl.pallas_call(functools.partial(copy_kernel, count), out_shape=tuple((ja...  2.74 us

profile of v3, /device:TPU:24, one launch (start us, length us, event | category | flops | bytes accessed | tf_op | source)
XLA Modules:
  0.0 82.2 jit_solution(17348233757142408296)
XLA Ops:
  0.6 78.8 %hyena.1 = (bf16[1,128,2048]{2,1,0:T(8,128)(2,1)}, bf16[1,128,2048]{2,1,0:T(8,128)(2,1)}, bf16[1,128,2048]{2,1,0:T(8,128)(2,1)}, f32[2048,128]{1,0:T(8,128)}) custom-call(bf16[1,128,2048]{2,1,0:T(8,128)(2,1)} %u_ref.1, bf16[1,128,2048]{2,1,0:T(8,128)(2,1)} %g_ref.1, bf16[1,128,2048]{2,1,0:T(8,128)(2,1)} %du_ref.1, f32[2048,128]{1,0:T(8,128)} %h_ref.1, ...), custom_call_target="tpu_custom_call" | custom-call | tf_op jit(solution)/shard_map/hyena/pallas_call | solution.py:486
  79.4 2.7 %results.1 = (bf16[1,128,2048]{2,1,0:T(8,128)(2,1)}, bf16[1,128,2048]{2,1,0:T(8,128)(2,1)}, bf16[1,128,2048]{2,1,0:T(8,128)(2,1)}, f32[2048,128]{1,0:T(8,128)}) custom-call(bf16[1,128,2048]{2,1,0:T(8,128)(2,1)} %get-tuple-element.12.refs_0_, bf16[1,128,2048]{2,1,0:T(8,128)(2,1)} %get-tuple-element.13.refs_1_, ...), custom_call_target="tpu_custom_call" | custom-call | tf_op jit(solution)/shard_map/results/pallas_call | solution.py:540

commit v4 on v3

--- a/solution.py
+++ b/solution.py
@@ -115,6 +115,25 @@
 SUBS = 2
 
 
+def encode(total, index, piece, value):
+    top = jnp.max(jnp.abs(value), axis=0, keepdims=True).astype(jnp.bfloat16)
+    size = top.astype(jnp.float32)
+    scaled = value * jnp.where(size > 0.0, 1.0 / size, 0.0)
+    fourth = (scaled * scaled) * (scaled * scaled) * 2.0**60
+    code = fourth * fourth
+    code = jnp.where(scaled < 0.0, -code, code)
+    total[index, piece, : value.shape[0]] = code.astype(jnp.bfloat16)
+    total[index, piece, value.shape[0] :] = jnp.broadcast_to(top, (16, top.shape[1]))
+
+
+def decoded(total, index, piece):
+    rows = total.shape[2] - 16
+    code = total[index, piece, :rows].astype(jnp.float32)
+    size = total[index, piece, rows:].astype(jnp.float32)[0:1]
+    root = jnp.sqrt(jnp.sqrt(jnp.sqrt(jnp.abs(code)) * 2.0**-60))
+    return jnp.where(code < 0.0, -root, root) * size
+
+
 def fused_kernel(
     n, rings, scale,
     u_ref, g_ref, du_ref, h_ref, analysis_ref, synthesis_ref, edge, back,
@@ -122,7 +141,7 @@
     arrive, leave, impulse, analysis, synthesis, signal, spec, prod, rim, rim_spec, rim_mix, rim_out,
     part, right_box, left_box, right_leaf, left_leaf, landing, total,
     table_sem, local_sem, in_send, in_recv, out_send, out_recv, sum_send, sum_recv, leaf_send, leaf_recv, land_send, land_recv,
-    all_send, all_recv, near_send, near_recv, twin_send, twin_recv,
+    all_send, all_recv, near_send, near_recv, twin_sem,
 ):
     me, dp = lax.axis_index("ctx"), lax.axis_index("dp")
     z, x = lax.div(dp, 2), lax.rem(dp, 2)
@@ -417,51 +436,53 @@
         for rail in range(2):
             landed(kind, rail)
         mine_sum = mine_sum + (landing[kind, 0] + landing[kind, 1])
-    total[z, kept] = mine_sum
-
-    shared = []
-
-    def spread(side, step, last_chain):
+    encode(total, z, x, mine_sum)
+
+    streams = (x, 1 - x)
+
+    def spread(side, step, i, last_chain):
         index = place(z - 2 * step) if side == 0 else place(z + 2 * step)
         two, one = ((up_two, up), (down_two, down))[side]
-        here = total.at[index, kept]
+        here = total.at[index, streams[i]]
         first = None
         if not last_chain:
-            first = hop(here, here, all_send.at[side, step], all_recv.at[side, step], two)
-        second = hop(here, here, near_send.at[side, step], near_recv.at[side, step], one)
-        if side == 0 or step:
-            share(index)
-        return first, second
-
-    def share(index):
-        here = total.at[index, kept]
-        i = len(shared)
-        shared.append(hop(here, here, twin_send.at[i], twin_recv.at[i], twin))
-
-    right, right_near = spread(0, 0, False)
-    left, left_near = spread(1, 0, False)
+            first = hop(here, here, all_send.at[side, step, i], all_recv.at[side, step, i], two)
+        return first, hop(here, here, near_send.at[side, step, i], near_recv.at[side, step, i], one)
+
+    def decode(q):
+        for part_of in range(2):
+            grad_ref[pl.ds(q + part_of * half * SPLIT, half, stride=SPLIT), :] = decoded(total, q, part_of) * scale
+
+    here = total.at[z, x]
+    swap = hop(here, here, twin_sem.at[0], twin_sem.at[1], twin)
+    far, near = {}, {}
+    for i in range(2):
+        if i:
+            swap.wait_recv()
+        for side in range(2):
+            far[side, i], near[side, i] = spread(side, 0, i, False)
     finish(DU)
     send_out(DU)
+    decode(z)
     for step in range(1, steps):
-        behind = (right_near, left_near)
-        right.wait_recv()
-        right, right_near = spread(0, step, False)
-        left.wait_recv()
-        left, left_near = spread(1, step, step == steps - 1)
-        behind[0].wait_recv()
-        share(place(z - 2 * step + 1))
-        behind[1].wait_recv()
-        share(place(z + 2 * step - 1))
-    right.wait_recv()
-    share(place(z - 2 * steps))
-    right_near.wait_recv()
-    share(place(z - 2 * steps + 1))
-    left_near.wait_recv()
-    share(place(z + 2 * steps - 1))
-    for copy in shared:
-        copy.wait_recv()
-    for q in range(SPLIT):
-        grad_ref[pl.ds(q, rows, stride=SPLIT), :] = total[q] * scale
+        behind = dict(near)
+        for i in range(2):
+            for side in range(2):
+                far[side, i].wait_recv()
+                far[side, i], near[side, i] = spread(side, step, i, side == 1 and step == steps - 1)
+        decode(place(z - 2 * step))
+        decode(place(z + 2 * step))
+        for side in range(2):
+            for i in range(2):
+                behind[side, i].wait_recv()
+            decode(place(z - 2 * step + 1) if side == 0 else place(z + 2 * step - 1))
+    for i in range(2):
+        far[0, i].wait_recv()
+    decode(place(z - 2 * steps))
+    for side in range(2):
+        for i in range(2):
+            near[side, i].wait_recv()
+        decode(place(z - 2 * steps + 1) if side == 0 else place(z + 2 * steps - 1))
     for copy in started + sent:
         copy.wait_send()
     for copy in finished:
@@ -507,11 +528,11 @@
             space(steps - 1, rows, width),
             space(steps - 1, rows, width),
             space(5, 2, rows // 2, width),
-            space(rings, rows, width),
+            space(rings, 2, rows // 2 + 16, width, kind=half),
             sem((3,)), sem((6,)),
             sem((3, n)), sem((3, n)), sem((3, n)), sem((3, n)),
             sem((2, steps, SUBS)), sem((2, steps, SUBS)), sem((2, steps)), sem((2, steps)), sem((5, 2)), sem((5, 2)),
-            sem((2, steps)), sem((2, steps)), sem((2, steps)), sem((2, steps)), sem((rings,)), sem((rings,)),
+            sem((2, steps, 2)), sem((2, steps, 2)), sem((2, steps, 2)), sem((2, steps, 2)), sem((2,)),
         ],
         compiler_params=pltpu.CompilerParams(
             collective_id=0, has_side_effects=True, vmem_limit_bytes=60 * MIB
@@ -523,13 +544,19 @@
 def copy_kernel(count, *refs):
     sources, targets, staged = refs[:count], refs[count : 2 * count], refs[2 * count : 3 * count]
     read_sem, write_sem = refs[3 * count :]
-    reads = [pltpu.make_async_copy(sources[i], staged[i], read_sem.at[i]) for i in range(count)]
-    writes = [pltpu.make_async_copy(staged[i], targets[i], write_sem.at[i]) for i in range(count)]
+    reads, writes = [], []
+    for i in range(count):
+        for piece in range(2):
+            size = sources[i].shape[-2] // 2
+            cut = (0,) * (len(sources[i].shape) - 2) + (pl.ds(piece * size, size),)
+            source, middle, target = sources[i].at[cut], staged[i].at[cut], targets[i].at[cut]
+            reads.append(pltpu.make_async_copy(source, middle, read_sem.at[i, piece]))
+            writes.append(pltpu.make_async_copy(middle, target, write_sem.at[i, piece]))
     for copy in reads:
         copy.start()
-    for i in range(count):
-        reads[i].wait()
-        writes[i].start()
+    for read, write in zip(reads, writes):
+        read.wait()
+        write.start()
     for copy in writes:
         copy.wait()
 
@@ -543,7 +570,7 @@
         in_specs=[anywhere] * count,
         out_specs=(anywhere,) * count,
         scratch_shapes=[pltpu.VMEM(a.shape, a.dtype) for a in arrays]
-        + [pltpu.SemaphoreType.DMA((count,)), pltpu.SemaphoreType.DMA((count,))],
+        + [pltpu.SemaphoreType.DMA((count, 2)), pltpu.SemaphoreType.DMA((count, 2))],
         compiler_params=pltpu.CompilerParams(vmem_limit_bytes=60 * MIB),
         name="results",
     )(*arrays)

time: 83.2 us -> 80.2 us (0.964)
  the two profiles are of different devices: /device:TPU:24 before, /device:TPU:2 now
where the time goes in v4:
time: 80.2 us; the launch traced here: 79.9 us
  Pallas kernels  79.2 us (99%)
    pallas_call x1, Pallas kernels, fused(): pl.pallas_call(functools.partial(fused_kernel, n, rings, scale), out_shap...  76.6 us
    pallas_call x1, Pallas kernels, copied(): pl.pallas_call(functools.partial(copy_kernel, count), out_shape=tuple((ja...  2.63 us

profile of v4, /device:TPU:2, one launch (start us, length us, event | category | flops | bytes accessed | tf_op | source)
XLA Modules:
  0.0 79.9 jit_solution(15387249036534865863)
XLA Ops:
  0.6 76.6 %hyena.1 = (bf16[1,128,2048]{2,1,0:T(8,128)(2,1)}, bf16[1,128,2048]{2,1,0:T(8,128)(2,1)}, bf16[1,128,2048]{2,1,0:T(8,128)(2,1)}, f32[2048,128]{1,0:T(8,128)}) custom-call(bf16[1,128,2048]{2,1,0:T(8,128)(2,1)} %u_ref.1, bf16[1,128,2048]{2,1,0:T(8,128)(2,1)} %g_ref.1, bf16[1,128,2048]{2,1,0:T(8,128)(2,1)} %du_ref.1, f32[2048,128]{1,0:T(8,128)} %h_ref.1, ...), custom_call_target="tpu_custom_call" | custom-call | tf_op jit(solution)/shard_map/hyena/pallas_call | solution.py:507
  77.2 2.6 %results.1 = (bf16[1,128,2048]{2,1,0:T(8,128)(2,1)}, bf16[1,128,2048]{2,1,0:T(8,128)(2,1)}, bf16[1,128,2048]{2,1,0:T(8,128)(2,1)}, f32[2048,128]{1,0:T(8,128)}) custom-call(bf16[1,128,2048]{2,1,0:T(8,128)(2,1)} %get-tuple-element.12.refs_0_, bf16[1,128,2048]{2,1,0:T(8,128)(2,1)} %get-tuple-element.13.refs_1_, ...), custom_call_target="tpu_custom_call" | custom-call | tf_op jit(solution)/shard_map/results/pallas_call | solution.py:567

commit v5 on v4

--- a/solution.py
+++ b/solution.py
@@ -363,9 +363,8 @@
         return carry
 
     lax.fori_loop(1, rings - 2, others, 0, unroll=rings - 3)
-    for i in range(1, steps - 1):
-        left_leaves.append(leaf(1, i))
-        right_leaves.append(leaf(0, i))
+    left_leaves.append(leaf(1, 1))
+    right_leaves.append(leaf(0, 1))
 
     def sum_left(step, left):
         left_leaves[step].wait_recv()
@@ -410,26 +409,26 @@
             device_id=twin, device_id_type=MESH,
         ).wait_recv()
 
+    send_in(DU)
+    left = sum_left(0, None)
+    right = sum_right(1, right)
+    left_leaves.append(leaf(1, 2))
+    right_leaves.append(leaf(0, 2))
+    mix(U, H, U, False, True, False)
+    finish(U)
+    left = sum_left(1, left)
+    right = sum_right(2, right)
     gift = hop(part.at[z, given], landing.at[4, 0], land_send.at[4, 0], land_recv.at[4, 0], twin)
     land(2, 1, lambda c: part.at[place(z + 1), c])
     land(3, rings - 1, lambda c: part.at[place(z - 1), c])
-    send_in(DU)
-    left = sum_left(0, None)
-    right = sum_right(1, right)
-    mix(U, H, U, False, True, False)
-    finish(U)
     send_out(U)
-    left = sum_left(1, left)
-    right = sum_right(2, right)
     mix(G, H, G, True, True, False)
-    finish(G)
-    send_out(G)
     sum_left(2, left)
     sum_right(3, right)
+    finish(G)
     receive(DU)
     load(DU)
     analyse(DU, (DU,))
-    mix(DU, H, DU, False, False, False)
     gift.wait_recv()
     mine_sum = part[z, kept] + landing[4, 0]
     for kind in (2, 3, 1, 0):
@@ -461,8 +460,8 @@
             swap.wait_recv()
         for side in range(2):
             far[side, i], near[side, i] = spread(side, 0, i, False)
-    finish(DU)
-    send_out(DU)
+    send_out(G)
+    mix(DU, H, DU, False, False, False)
     decode(z)
     for step in range(1, steps):
         behind = dict(near)
@@ -470,6 +469,9 @@
             for side in range(2):
                 far[side, i].wait_recv()
                 far[side, i], near[side, i] = spread(side, step, i, side == 1 and step == steps - 1)
+        if step == 1:
+            finish(DU)
+            send_out(DU)
         decode(place(z - 2 * step))
         decode(place(z + 2 * step))
         for side in range(2):

time: 80.2 us -> 78.8 us (0.983)
  the two profiles are of different devices: /device:TPU:2 before, /device:TPU:4 now
where the time goes in v5:
time: 78.8 us; the launch traced here: 78.6 us
  Pallas kernels  77.9 us (99%)
    pallas_call x1, Pallas kernels, fused(): pl.pallas_call(functools.partial(fused_kernel, n, rings, scale), out_shap...  75.3 us
    pallas_call x1, Pallas kernels, copied(): pl.pallas_call(functools.partial(copy_kernel, count), out_shape=tuple((ja...  2.63 us

profile of v5, /device:TPU:4, one launch (start us, length us, event | category | flops | bytes accessed | tf_op | source)
XLA Modules:
  0.0 78.6 jit_solution(8689103615756976989)
XLA Ops:
  0.6 75.3 %hyena.1 = (bf16[1,128,2048]{2,1,0:T(8,128)(2,1)}, bf16[1,128,2048]{2,1,0:T(8,128)(2,1)}, bf16[1,128,2048]{2,1,0:T(8,128)(2,1)}, f32[2048,128]{1,0:T(8,128)}) custom-call(bf16[1,128,2048]{2,1,0:T(8,128)(2,1)} %u_ref.1, bf16[1,128,2048]{2,1,0:T(8,128)(2,1)} %g_ref.1, bf16[1,128,2048]{2,1,0:T(8,128)(2,1)} %du_ref.1, f32[2048,128]{1,0:T(8,128)} %h_ref.1, ...), custom_call_target="tpu_custom_call" | custom-call | tf_op jit(solution)/shard_map/hyena/pallas_call | solution.py:509
  75.9 2.6 %results.1 = (bf16[1,128,2048]{2,1,0:T(8,128)(2,1)}, bf16[1,128,2048]{2,1,0:T(8,128)(2,1)}, bf16[1,128,2048]{2,1,0:T(8,128)(2,1)}, f32[2048,128]{1,0:T(8,128)}) custom-call(bf16[1,128,2048]{2,1,0:T(8,128)(2,1)} %get-tuple-element.12.refs_0_, bf16[1,128,2048]{2,1,0:T(8,128)(2,1)} %get-tuple-element.13.refs_1_, ...), custom_call_target="tpu_custom_call" | custom-call | tf_op jit(solution)/shard_map/results/pallas_call | solution.py:569

commit v6 on v5

--- a/solution.py
+++ b/solution.py
@@ -164,8 +164,6 @@
         pltpu.make_async_copy(src, dst, table_sem.at[i])
         for i, (src, dst) in enumerate(((h_ref, impulse), (analysis_ref, analysis), (synthesis_ref, synthesis)))
     ]
-    for copy in tables:
-        copy.start()
     barrier = pltpu.get_barrier_semaphore()
     for step in range(1, n):
         pl.semaphore_signal(
@@ -173,6 +171,8 @@
         )
     for device in (up, up_two, down, down_two, twin, *around):
         pl.semaphore_signal(barrier, inc=1, device_id=device, device_id_type=MESH)
+    for copy in tables:
+        copy.start()
     pl.semaphore_wait(barrier, n + 8)
 
     remote, sent, locals_ = {}, [], {}
@@ -265,7 +265,7 @@
                 prod[o, q, lower, :] = points[q][1]
             return carry
 
-        lax.fori_loop(0, rows // 8, body, 0)
+        lax.fori_loop(0, rows // 8, body, 0, unroll=2)
 
     def turn(s):
         def body(tile, carry):
@@ -277,7 +277,7 @@
                 spec[s, j, lower, :] = points[j][1]
             return carry
 
-        lax.fori_loop(0, rows // 8, body, 0)
+        lax.fori_loop(0, rows // 8, body, 0, unroll=2)
 
     def residue(o, q):
         prod[o, q, 0:1, :] = rim_out[o, pl.ds(q, 1), :]

time: 78.8 us -> 78.3 us (level)
  the two profiles are of different devices: /device:TPU:4 before, /device:TPU:24 now
where the time goes in v6:
time: 78.3 us; the launch traced here: 77.1 us
  Pallas kernels  76.4 us (98%)
    pallas_call x1, Pallas kernels, fused(): pl.pallas_call(functools.partial(fused_kernel, n, rings, scale), out_shap...  73.8 us
    pallas_call x1, Pallas kernels, copied(): pl.pallas_call(functools.partial(copy_kernel, count), out_shape=tuple((ja...  2.63 us

profile of v6, /device:TPU:24, one launch (start us, length us, event | category | flops | bytes accessed | tf_op | source)
XLA Modules:
  0.0 77.1 jit_solution(10646942593593260854)
XLA Ops:
  0.6 73.8 %hyena.1 = (bf16[1,128,2048]{2,1,0:T(8,128)(2,1)}, bf16[1,128,2048]{2,1,0:T(8,128)(2,1)}, bf16[1,128,2048]{2,1,0:T(8,128)(2,1)}, f32[2048,128]{1,0:T(8,128)}) custom-call(bf16[1,128,2048]{2,1,0:T(8,128)(2,1)} %u_ref.1, bf16[1,128,2048]{2,1,0:T(8,128)(2,1)} %g_ref.1, bf16[1,128,2048]{2,1,0:T(8,128)(2,1)} %du_ref.1, f32[2048,128]{1,0:T(8,128)} %h_ref.1, ...), custom_call_target="tpu_custom_call" | custom-call | tf_op jit(solution)/shard_map/hyena/pallas_call | solution.py:509
  74.4 2.6 %results.1 = (bf16[1,128,2048]{2,1,0:T(8,128)(2,1)}, bf16[1,128,2048]{2,1,0:T(8,128)(2,1)}, bf16[1,128,2048]{2,1,0:T(8,128)(2,1)}, f32[2048,128]{1,0:T(8,128)}) custom-call(bf16[1,128,2048]{2,1,0:T(8,128)(2,1)} %get-tuple-element.12.refs_0_, bf16[1,128,2048]{2,1,0:T(8,128)(2,1)} %get-tuple-element.13.refs_1_, ...), custom_call_target="tpu_custom_call" | custom-call | tf_op jit(solution)/shard_map/results/pallas_call | solution.py:569
